TPU v7x, 512 devices: a whole 4x8x8 slice. The times are simulated.
512 devices in a mesh: tm: 32 (over x, y), space: 16 (over z, core).
Axes of the slice: x: 4, y: 8, z: 8, core: 2. Of those that a mesh axis runs over, the one named last changes fastest.
Arguments:
- frames: bfloat16 [64, 16, 16, 32, 256], P('tm', 'space'), may hold values from -60 to 60
- norm_gain: float32 [256], replicated, may hold values from 0.1 to 1.9
- norm_shift: float32 [256], replicated, may hold values from -3 to 3
- conv_filter: bfloat16 [3, 3, 3, 256, 256], replicated, may hold values from -0.078125 to 0.078125
- conv_offset: float32 [256], replicated, may hold values from -3 to 3
Outputs:
- block_out: bfloat16 [64, 16, 16, 32, 256], P('tm', 'space')
All inputs are finite; a program needn't handle non-finite values.
Results may differ from a plain program's by a relative error of at most 0.0015.
The roundings to bfloat16 on the way count: a program that leaves them out, or rounds other values in their place, can miss the bound.
Values may be sent and summed in bfloat16 or wider, within the bound.
No kernel may reach another device: no remote copies, remote signals or barrier semaphores. Data moves between devices by JAX's collectives and lax.ppermute only.
A program may use at most 64 MiB of HBM per device.

v0:
```python
import jax
import jax.numpy as jnp
from jax import lax
from jax.sharding import PartitionSpec as P

GROUPS = 32


def prefix(value, axis, join, neutral):
    count, mine = (lax.axis_size(axis), lax.axis_index(axis))
    pieces = jax.tree.map(lambda part: lax.all_gather(part, axis), value)
    running = jax.tree.map(
        lambda part, zero: jnp.full_like(part, 0) + jnp.asarray(zero, part.dtype), value, neutral
    )

    def hop(position, running):
        longer = join(running, jax.tree.map(lambda part: part[position], pieces))
        return jax.tree.map(lambda new, old: jnp.where(position < mine, new, old), longer, running)

    return lax.fori_loop(0, count - 1, hop, running)


def shifted_2(value, axis, steps):
    count = lax.axis_size(axis)
    initial, last = (max(0, -steps), min(count, count - steps))
    return lax.ppermute(value, axis, [(source, source + steps) for source in range(initial, last)])


def add_pair(earlier, later):
    return (earlier[0] + later[0], earlier[1] + later[1])


def causal_norm(values, gain, shift):
    frames_here, height, width, channels = values.shape
    width_group = channels // GROUPS
    plain = jnp.sum(values, axis=(1, 2)).reshape(frames_here, GROUPS, width_group).sum(-1)
    square = jnp.sum(values * values, axis=(1, 2)).reshape(frames_here, GROUPS, width_group).sum(-1)
    plain, square = lax.psum((plain, square), "space")
    run_plain = jnp.cumsum(plain, axis=0)
    run_square = jnp.cumsum(square, axis=0)
    empty = jnp.zeros((GROUPS,), jnp.float32)
    start_plain, start_square = prefix(
        (run_plain[-1], run_square[-1]), "tm", add_pair, (empty, empty)
    )
    run_plain = run_plain + start_plain
    run_square = run_square + start_square
    first_frame = lax.axis_index("tm") * frames_here
    cells = height * width * lax.axis_size("space") * width_group
    count = (first_frame + jnp.arange(frames_here, dtype=jnp.int32) + 1).astype(jnp.float32) * cells
    mean = run_plain / count[:, None]
    spread = run_square / count[:, None] - mean * mean
    inverse = lax.rsqrt(spread + 1e-06)
    mean_wide = jnp.repeat(mean, width_group, axis=1)
    inverse_wide = jnp.repeat(inverse, width_group, axis=1)
    normed = (values - mean_wide[:, None, None, :]) * inverse_wide[:, None, None, :] * gain + shift
    return jax.nn.silu(normed).astype(jnp.bfloat16)


def widen(slab):
    tiles = lax.axis_size("space")
    across = min(tiles, 4)
    column = lax.axis_index("space") % across
    has_left = column > 0
    has_right = column < across - 1
    from_left = shifted_2(slab[:, :, -1:], "space", 1)
    from_right = shifted_2(slab[:, :, :1], "space", -1)
    from_left = jnp.where(has_left, from_left, jnp.zeros_like(from_left))
    from_right = jnp.where(has_right, from_right, jnp.zeros_like(from_right))
    middle = jnp.concatenate([from_left, slab, from_right], axis=2)
    top = shifted_2(middle[:, -1:], "space", across)
    bottom = shifted_2(middle[:, :1], "space", -across)
    return jnp.concatenate([top, middle, bottom], axis=1)


def apply_taps(padded, kernel):
    frames_all, rows_all, cols_all, channels = padded.shape
    frames_here = frames_all - 2
    height = rows_all - 2
    width = cols_all - 2
    outputs = kernel.shape[4]
    shifted = jnp.concatenate(
        [padded[:, :, offset : offset + width, :] for offset in range(3)], axis=3
    )
    total = jnp.zeros((frames_here * height * width, outputs), jnp.float32)
    for lagged in range(3):
        for vertical in range(3):
            window = shifted[lagged : lagged + frames_here, vertical : vertical + height]
            window = window.reshape(frames_here * height * width, 3 * channels)
            total = total + jnp.dot(
                window,
                kernel[lagged, vertical].reshape(3 * channels, outputs),
                preferred_element_type=jnp.float32,
            )
    return total.reshape(frames_here, height, width, outputs)


def causal_conv(active, kernel, offset):
    past = shifted_2(active, "tm", 1)
    padded = widen(jnp.concatenate([past, active], axis=0))
    return apply_taps(padded, kernel) + offset


def local(frames, norm_gain, norm_shift, conv_filter, conv_offset):
    inputs = frames[:, 0].astype(jnp.float32)
    act = causal_norm(inputs, norm_gain, norm_shift)
    output = (inputs + causal_conv(act, conv_filter, conv_offset)).astype(jnp.bfloat16)
    return output[:, None]


def solution(mesh):
    placed = (P("tm", "space", None, None, None), P(), P(), P(), P())
    return jax.shard_map(
        local,
        mesh=mesh,
        in_specs=placed,
        out_specs=P("tm", "space", None, None, None),
        check_vma=False,
    )
```

profile of v0, /device:TPU:132, one launch (start us, length us, event | category | flops | bytes accessed | tf_op | source)
XLA Modules:
  0.0 146.4 jit_solution(6521616663395949460)
XLA Ops:
  0.0 1.2 convert_reduce_fusion
  1.2 1.2 fusion.2
  2.4 0.1 reshape.61
  2.5 0.1 reshape.62
  2.6 0.1 reduce_sum.37
  2.7 0.1 reduce_sum.39
  2.8 24.4 %all-reduce = (f32[2,32]{1,0:T(2,128)S(1)}, f32[2,32]{1,0:T(2,128)S(1)}) all-reduce(f32[2,32]{1,0:T(2,128)S(1)} %reduce_sum.37, f32[2,32]{1,0:T(2,128)S(1)} %reduce_sum.39), channel_id=1, replica_groups=mesh['tm'=32,'space'=16] {'space'}, use_global_device_ids=true, to_apply=%region_2.0 | all-reduce | flops 128 | bytes 1024 | tf_op jit(solution)/shard_map/psum | solution.py:38
  27.2 34.7 %all-gather = f32[32,1,32]{2,1,0:T(1,128)S(1)} all-gather(f32[1,1,32]{2,1,0:T(1,128)S(1)} %slice_bitcast_fusion.1), channel_id=1, replica_groups=mesh['tm'=32,'space'=16] {'tm'}, dimensions={0}, use_global_device_ids=true | all-gather | bytes 4224 | tf_op jit(solution)/shard_map/all_gather | solution.py:11
  61.9 34.3 %all-gather.1 = f32[32,1,32]{2,1,0:T(1,128)S(1)} all-gather(f32[1,1,32]{2,1,0:T(1,128)S(1)} %slice_bitcast_fusion), channel_id=1, replica_groups=mesh['tm'=32,'space'=16] {'tm'}, dimensions={0}, use_global_device_ids=true | all-gather | bytes 4224 | tf_op jit(solution)/shard_map/all_gather | solution.py:11
  96.2 1.3 while.16
  97.5 0.1 add_rsqrt_fusion
  97.6 0.1 broadcast_in_dim.8
  97.7 0.1 mul.42
  97.8 0.1 broadcast_in_dim.7
  97.8 0.1 sub.13
  97.9 0.0 copy-done
  98.0 0.4 fusion.11
  98.3 1.9 %collective-permute-start = (bf16[2,16,32,256]{3,2,1,0:T(8,128)(2,1)S(1)}, bf16[2,16,32,256]{3,2,1,0:T(8,128)(2,1)S(1)}, u32[]{:S(2)}, u32[]{:S(2)}) collective-permute-start(bf16[2,16,32,256]{3,2,1,0:T(8,128)(2,1)S(1)} %fusion.11), channel_id=1, source_target_pairs={{0,16},{16,32},{32,48},{48,64},{64,80},{80,96},{96,112},{112,128},... | collective-permute-start | bytes 1572872 | tf_op jit(solution)/shard_map/ppermute | solution.py:26
  100.3 11.2 %collective-permute-done = bf16[2,16,32,256]{3,2,1,0:T(8,128)(2,1)S(1)} collective-permute-done((bf16[2,16,32,256]{3,2,1,0:T(8,128)(2,1)S(1)}, bf16[2,16,32,256]{3,2,1,0:T(8,128)(2,1)S(1)}, u32[]{:S(2)}, u32[]{:S(2)}) %collective-permute-start) | collective-permute-done | bytes 524320 | tf_op jit(solution)/shard_map/ppermute | solution.py:26
  111.5 0.1 pad_maximum_fusion.7
  111.6 1.9 %collective-permute-start.1 = (bf16[4,16,1,256]{3,2,1,0:T(2,128)(2,1)S(1)}, bf16[4,16,1,256]{3,2,1,0:T(2,128)(2,1)S(1)}, u32[]{:S(2)}, u32[]{:S(2)}) collective-permute-start(bf16[4,16,1,256]{3,2,1,0:T(2,128)(2,1)S(1)} %get-tuple-element.179), channel_id=1, source_target_pairs={{0,1},{1,2},{2,3},{3,4},{4,5},{5,6},{6,7},{7,8},{8,9},{9,10},{10,1... | collective-permute-start | bytes 98312 | tf_op jit(solution)/shard_map/ppermute | solution.py:26
  113.6 3.6 %collective-permute-start.2 = (bf16[4,16,1,256]{3,2,1,0:T(2,128)(2,1)S(1)}, bf16[4,16,1,256]{3,2,1,0:T(2,128)(2,1)S(1)}, u32[]{:S(2)}, u32[]{:S(2)}) collective-permute-start(bf16[4,16,1,256]{3,2,1,0:T(2,128)(2,1)S(1)} %get-tuple-element.180), channel_id=1, source_target_pairs={{1,0},{2,1},{3,2},{4,3},{5,4},{6,5},{7,6},{8,7},{9,8},{10,9},{11,1... | collective-permute-start | bytes 98312 | tf_op jit(solution)/shard_map/ppermute | solution.py:26
  117.2 0.0 collective-permute-done.1
  117.2 0.1 broadcast_select_fusion.5
  117.3 1.8 %collective-permute-done.2 = bf16[4,16,1,256]{3,2,1,0:T(2,128)(2,1)S(1)} collective-permute-done((bf16[4,16,1,256]{3,2,1,0:T(2,128)(2,1)S(1)}, bf16[4,16,1,256]{3,2,1,0:T(2,128)(2,1)S(1)}, u32[]{:S(2)}, u32[]{:S(2)}) %collective-permute-start.2) | collective-permute-done | bytes 32800 | tf_op jit(solution)/shard_map/ppermute | solution.py:26
  119.1 0.1 broadcast_select_fusion.4
  119.2 0.1 pad_maximum_fusion.5
  119.3 7.8 %collective-permute-start.3 = (bf16[4,1,34,256]{3,2,1,0:T(8,128)(2,1)S(1)}, bf16[4,1,34,256]{3,2,1,0:T(8,128)(2,1)S(1)}, u32[]{:S(2)}, u32[]{:S(2)}) collective-permute-start(bf16[4,1,34,256]{3,2,1,0:T(8,128)(2,1)S(1)} %get-tuple-element.177), channel_id=1, source_target_pairs={{0,4},{1,5},{2,6},{3,7},{4,8},{5,9},{6,10},{7,11},{8,12},{9,13},{1... | collective-permute-start | bytes 208904 | tf_op jit(solution)/shard_map/ppermute | solution.py:26
  127.0 1.9 %collective-permute-start.4 = (bf16[4,1,34,256]{3,2,1,0:T(8,128)(2,1)S(1)}, bf16[4,1,34,256]{3,2,1,0:T(8,128)(2,1)S(1)}, u32[]{:S(2)}, u32[]{:S(2)}) collective-permute-start(bf16[4,1,34,256]{3,2,1,0:T(8,128)(2,1)S(1)} %get-tuple-element.178), channel_id=1, source_target_pairs={{4,0},{5,1},{6,2},{7,3},{8,4},{9,5},{10,6},{11,7},{12,8},{13,9},{1... | collective-permute-start | bytes 208904 | tf_op jit(solution)/shard_map/ppermute | solution.py:26
  129.0 2.3 %fusion.13 = (bf16[1,1,3,256,256]{4,3,2,1,0:T(8,128)(2,1)S(1)}, bf16[1,1,3,256,256]{4,3,2,1,0:T(8,128)(2,1)S(1)}, bf16[1,1,3,256,256]{4,3,2,1,0:T(8,128)(2,1)S(1...) fusion(bf16[3,3,3,256,256]{4,3,2,1,0:T(8,128)(2,1)} %param.10), kind=kLoop, calls=%fused_computation.44 | loop fusion | bytes 7077888 | tf_op jit(solution)/shard_map/slice | solution.py:91
  131.3 0.0 collective-permute-done.3
  131.3 5.0 %collective-permute-done.4 = bf16[4,1,34,256]{3,2,1,0:T(8,128)(2,1)S(1)} collective-permute-done((bf16[4,1,34,256]{3,2,1,0:T(8,128)(2,1)S(1)}, bf16[4,1,34,256]{3,2,1,0:T(8,128)(2,1)S(1)}, u32[]{:S(2)}, u32[]{:S(2)}) %collective-permute-start.4) | collective-permute-done | bytes 69664 | tf_op jit(solution)/shard_map/ppermute | solution.py:26
  136.3 0.9 pad_maximum_fusion.1
  137.2 0.9 fusion.15
  138.1 0.3 pad_maximum_fusion
  138.4 1.6 %fusion.14 = (bf16[2,16,32,768]{3,2,1,0:T(8,128)(2,1)S(1)}, bf16[2,16,32,768]{3,2,1,0:T(8,128)(2,1)S(1)}, bf16[2,16,32,768]{3,2,1,0:T(8,128)(2,1)S(1)}, bf16[2,1...) fusion(bf16[4,18,32,768]{3,2,1,0:T(8,128)(2,1)S(1)} %pad_maximu, ...), kind=kLoop, calls=%fused_computation.45 | loop fusion | bytes 28311552 | tf_op jit(solution)/shard_map/slice | solution.py:87
  140.0 0.6 fusion.16
  140.6 0.6 convolution_add_fusion.7
  141.2 0.6 convolution_add_fusion.6
  141.8 0.6 convolution_add_fusion.5
  142.4 0.6 convolution_add_fusion.4
  143.0 0.6 convolution_add_fusion.3
  143.5 0.6 convolution_add_fusion.2
  144.1 0.6 convolution_add_fusion.1
  144.7 0.0 copy-start.1
  144.7 0.6 convolution_add_fusion
  145.3 0.1 copy-done.1
  145.4 1.0 fusion.12
  (43 shorter events, 0.7 us)
Async XLA Ops:
  0.0 97.9 %copy-start = (bf16[2,1,16,32,256]{4,3,2,1,0:T(8,128)(2,1)S(1)}, bf16[2,1,16,32,256]{4,3,2,1,0:T(8,128)(2,1)}, u32[]{:S(2)}) copy-start(bf16[2,1,16,32,256]{4,3,2,1,0:T(8,128)(2,1)} %param.7) | copy-start | bytes 1572868
  0.0 97.9 %copy-start.3 = (f32[256]{0:T(256)S(1)}, f32[256]{0:T(256)}, u32[]{:S(2)}) copy-start(f32[256]{0:T(256)} %param.8) | copy-start | bytes 3076
  0.0 98.0 %copy-start.2 = (f32[256]{0:T(256)S(1)}, f32[256]{0:T(256)}, u32[]{:S(2)}) copy-start(f32[256]{0:T(256)} %param.9) | copy-start | bytes 3076
  98.3 13.2 %collective-permute-start = (bf16[2,16,32,256]{3,2,1,0:T(8,128)(2,1)S(1)}, bf16[2,16,32,256]{3,2,1,0:T(8,128)(2,1)S(1)}, u32[]{:S(2)}, u32[]{:S(2)}) collective-permute-start(bf16[2,16,32,256]{3,2,1,0:T(8,128)(2,1)S(1)} %fusion.11), channel_id=1, source_target_pairs={{0,16},{16,32},{32,48},{48,64},{64,80},{80,96},{96,112},{112,128},... | collective-permute-start | bytes 1572872 | tf_op jit(solution)/shard_map/ppermute | solution.py:26
  111.6 5.6 %collective-permute-start.1 = (bf16[4,16,1,256]{3,2,1,0:T(2,128)(2,1)S(1)}, bf16[4,16,1,256]{3,2,1,0:T(2,128)(2,1)S(1)}, u32[]{:S(2)}, u32[]{:S(2)}) collective-permute-start(bf16[4,16,1,256]{3,2,1,0:T(2,128)(2,1)S(1)} %get-tuple-element.179), channel_id=1, source_target_pairs={{0,1},{1,2},{2,3},{3,4},{4,5},{5,6},{6,7},{7,8},{8,9},{9,10},{10,1... | collective-permute-start | bytes 98312 | tf_op jit(solution)/shard_map/ppermute | solution.py:26
  113.6 5.5 %collective-permute-start.2 = (bf16[4,16,1,256]{3,2,1,0:T(2,128)(2,1)S(1)}, bf16[4,16,1,256]{3,2,1,0:T(2,128)(2,1)S(1)}, u32[]{:S(2)}, u32[]{:S(2)}) collective-permute-start(bf16[4,16,1,256]{3,2,1,0:T(2,128)(2,1)S(1)} %get-tuple-element.180), channel_id=1, source_target_pairs={{1,0},{2,1},{3,2},{4,3},{5,4},{6,5},{7,6},{8,7},{9,8},{10,9},{11,1... | collective-permute-start | bytes 98312 | tf_op jit(solution)/shard_map/ppermute | solution.py:26
  119.3 12.0 %collective-permute-start.3 = (bf16[4,1,34,256]{3,2,1,0:T(8,128)(2,1)S(1)}, bf16[4,1,34,256]{3,2,1,0:T(8,128)(2,1)S(1)}, u32[]{:S(2)}, u32[]{:S(2)}) collective-permute-start(bf16[4,1,34,256]{3,2,1,0:T(8,128)(2,1)S(1)} %get-tuple-element.177), channel_id=1, source_target_pairs={{0,4},{1,5},{2,6},{3,7},{4,8},{5,9},{6,10},{7,11},{8,12},{9,13},{1... | collective-permute-start | bytes 208904 | tf_op jit(solution)/shard_map/ppermute | solution.py:26
  127.0 9.2 %collective-permute-start.4 = (bf16[4,1,34,256]{3,2,1,0:T(8,128)(2,1)S(1)}, bf16[4,1,34,256]{3,2,1,0:T(8,128)(2,1)S(1)}, u32[]{:S(2)}, u32[]{:S(2)}) collective-permute-start(bf16[4,1,34,256]{3,2,1,0:T(8,128)(2,1)S(1)} %get-tuple-element.178), channel_id=1, source_target_pairs={{4,0},{5,1},{6,2},{7,3},{8,4},{9,5},{10,6},{11,7},{12,8},{13,9},{1... | collective-permute-start | bytes 208904 | tf_op jit(solution)/shard_map/ppermute | solution.py:26
  144.7 0.7 copy-start.1
where the time goes:
time: 147 us; the launch traced here: 146 us
  blocking collectives  93.3 us (63%)
  waiting for transfers between devices  18 us (12%)
  starting transfers between devices  17.2 us (12%)
  other arithmetic  6.13 us (4%)
  local copies, waits for them, and re-layouts  5.49 us (4%)
  matrix products  5.19 us (4%)
    all_gather x2, blocking collectives, prefix(): pieces = jax.tree.map(lambda part: lax.all_gather(part, axis), value)  69 us
    psum x1, blocking collectives, causal_norm(): plain, square = lax.psum((plain, square), 'space')  24.4 us
    ppermute x5, waiting for transfers between devices, shifted_2(): lax.ppermute(value, axis, [(source, source + steps) for source in range(i...  18 us
    ppermute x5, starting transfers between devices, shifted_2(): lax.ppermute(value, axis, [(source, source + steps) for source in range(i...  17.2 us
    dot_general x9, matrix products, apply_taps(): jnp.dot(window, kernel[lagged, vertical].reshape(3 * channels, outputs),...  5.19 us
  transfers between devices with their start and end apart: 5, of which 3 were waited for; matrix products, arithmetic and copies ran while one was open for 2% of the time, Pallas kernels for 0%

commit v1 on v0

v1 whole, which is shorter than its diff:
```python
import functools

import jax
import jax.numpy as jnp
from jax import lax
from jax.experimental import pallas as pl
from jax.experimental.pallas import tpu as pltpu
from jax.sharding import PartitionSpec as P

GROUPS = 32
ACROSS = 4
F32, BF16 = jnp.float32, jnp.bfloat16


def split(value):
    high = value.astype(BF16)
    rest = value - high.astype(F32)
    middle = rest.astype(BF16)
    low = (rest - middle.astype(F32)).astype(BF16)
    return high, middle, low


def exact_dot(value, table):
    return sum(jnp.dot(part, table, preferred_element_type=F32) for part in split(value))


def sums_kernel(frames_ref, out_ref):
    frames, height, width, channels = frames_ref.shape
    per_group = channels // GROUPS
    channel = lax.broadcasted_iota(jnp.int32, (channels, 128), 0)
    lane = lax.broadcasted_iota(jnp.int32, (channels, 128), 1)
    total = jnp.zeros((8, 128), F32)
    for frame in range(frames):
        plain = jnp.zeros((8, channels), F32)
        square = jnp.zeros((8, channels), F32)
        for row in range(height):
            block = frames_ref[frame, row].astype(F32).reshape(width // 8, 8, channels)
            plain = plain + block.sum(0)
            square = square + (block * block).sum(0)
        for kind, value in enumerate((plain, square)):
            slot = (kind * frames + frame) * GROUPS
            table = jnp.where(lane == slot + channel // per_group, 1.0, 0.0).astype(BF16)
            total = total + exact_dot(value, table)
    row = total.sum(0, keepdims=True)
    out_ref[...] = jnp.broadcast_to(row[None], out_ref.shape)


def group_sums(frames, peers):
    return pl.pallas_call(
        sums_kernel,
        out_shape=jax.ShapeDtypeStruct((peers, 1, 128), F32),
        in_specs=[pl.BlockSpec(memory_space=pltpu.VMEM)],
        out_specs=pl.BlockSpec(memory_space=pltpu.VMEM),
        cost_estimate=pl.CostEstimate(flops=1 << 20, bytes_accessed=1 << 19, transcendentals=0),
    )(frames)


def conv_kernel(place_ref, sums_ref, own_ref, past_ref, edge_ref, past_edge_ref, gain_ref, shift_ref, filter_ref,
                offset_ref, out_ref, shifted):
    frames, height, width, channels = own_ref.shape
    per_group = channels // GROUPS
    time, tile = place_ref[0], place_ref[1]
    tiles = place_ref[2]
    row_of, col_of = tile // ACROSS, tile % ACROSS
    down_max = tiles // ACROSS - 1

    sums = sums_ref[...]
    index = lax.broadcasted_iota(jnp.int32, sums.shape, 0)
    lane = lax.broadcasted_iota(jnp.int32, (1, 128), 1)
    first = jnp.where((lane // GROUPS) % 2 == 0, 1.0, 0.0).astype(F32)
    before = jnp.where(index < time - 1, sums, 0.0).sum(0, keepdims=True)
    past = jnp.where(index == time - 1, sums, 0.0).sum(0, keepdims=True)
    own = jnp.where(index == time, sums, 0.0).sum(0, keepdims=True)
    running = jnp.concatenate(
        [before + past * first, before + past, before + past + own * first, before + past + own]
        + [jnp.zeros((4, 128), F32)],
        axis=0,
    )
    slot = lax.broadcasted_iota(jnp.int32, (128, channels), 0)
    channel = lax.broadcasted_iota(jnp.int32, (128, channels), 1)
    wide = []
    for kind in range(2):
        table = (slot // (2 * GROUPS) == kind) & (slot % GROUPS == channel // per_group)
        wide.append(exact_dot(running, jnp.where(table, 1.0, 0.0).astype(BF16)))
    frame_row = lax.broadcasted_iota(jnp.int32, (8, channels), 0)
    cells = height * width * tiles * per_group
    count = jnp.maximum((time * 2 - 1 + frame_row) * cells, 1).astype(F32)
    mean = wide[0] / count
    spread = wide[1] / count - mean * mean
    scale = lax.rsqrt(spread + 1e-06) * gain_ref[...]
    shift = shift_ref[...]

    def activate(value, which):
        u = (value.astype(F32) - mean[which : which + 1]) * scale[which : which + 1] + shift
        return u / (1.0 + jnp.exp(-u))

    has_left = jnp.where(col_of > 0, 1.0, 0.0).astype(F32)
    has_right = jnp.where(col_of < ACROSS - 1, 1.0, 0.0).astype(F32)
    has_up = jnp.where(row_of > 0, 1.0, 0.0).astype(F32)
    has_down = jnp.where(row_of < down_max, 1.0, 0.0).astype(F32)
    has_past = jnp.where(time > 0, 1.0, 0.0).astype(F32)
    up_at = 2 * height
    down_at = up_at + width
    corner_at = down_at + width

    def put(which, row, center, left, right):
        at = pl.ds((which * (height + 2) + row) * width, width)
        place = lax.broadcasted_iota(jnp.int32, (width, channels), 0)
        toward = jnp.where(place == 0, left, pltpu.roll(center, 1, 0))
        away = jnp.where(place == width - 1, right, pltpu.roll(center, width - 1, 0))
        shifted[at, 0:channels] = toward.astype(BF16)
        shifted[at, channels : 2 * channels] = center.astype(BF16)
        shifted[at, 2 * channels : 3 * channels] = away.astype(BF16)

    for which in range(4):
        source = past_ref if which < 2 else own_ref
        edges = past_edge_ref if which < 2 else edge_ref
        here = has_past if which < 2 else jnp.ones((), F32)
        frame = which % 2
        left = activate(edges[frame, 0:height], which) * (has_left * here)
        right = activate(edges[frame, height : 2 * height], which) * (has_right * here)
        up = activate(edges[frame, up_at:down_at], which) * (has_up * here)
        down = activate(edges[frame, down_at:corner_at], which) * (has_down * here)
        corners = activate(edges[frame, corner_at : corner_at + 16], which) * here
        put(which, 0, up, corners[0:1] * (has_up * has_left), corners[1:2] * (has_up * has_right))
        put(which, height + 1, down, corners[2:3] * (has_down * has_left), corners[3:4] * (has_down * has_right))
        for row in range(height):
            center = activate(source[frame, row], which) * here
            put(which, row + 1, center, left[row : row + 1], right[row : row + 1])

    for frame in range(frames):
        total = jnp.zeros((height * width, channels), F32)
        for lagged in range(3):
            for vertical in range(3):
                at = ((frame + lagged) * (height + 2) + vertical) * width
                total = total + jnp.dot(
                    shifted[at : at + height * width, :],
                    filter_ref[lagged * 3 + vertical],
                    preferred_element_type=F32,
                )
        value = own_ref[frame].astype(F32).reshape(height * width, channels)
        value = value + (total + offset_ref[...])
        out_ref[frame] = value.astype(BF16).reshape(height, width, channels)


def convolve(place, sums, own, past, edge, past_edge, gain, shift, taps, offset):
    frames, height, width, channels = own.shape
    vmem = pl.BlockSpec(memory_space=pltpu.VMEM)
    return pl.pallas_call(
        conv_kernel,
        out_shape=jax.ShapeDtypeStruct(own.shape, BF16),
        in_specs=[pl.BlockSpec(memory_space=pltpu.SMEM)] + [vmem] * 9,
        out_specs=vmem,
        scratch_shapes=[
            pltpu.VMEM((4 * (height + 2) * width, 3 * channels), BF16),
        ],
        compiler_params=pltpu.CompilerParams(vmem_limit_bytes=40 << 20),
        cost_estimate=pl.CostEstimate(flops=4 << 30, bytes_accessed=6 << 20, transcendentals=1 << 20),
    )(place, sums, own, past, edge, past_edge, gain, shift, taps, offset)


def local(frames, norm_gain, norm_shift, conv_filter, conv_offset):
    own = frames[:, 0]
    count, height, width, channels = own.shape
    times, tiles = lax.axis_size("tm"), lax.axis_size("space")
    place = jnp.stack([lax.axis_index("tm"), lax.axis_index("space"), jnp.int32(tiles)]).astype(jnp.int32)

    later = [(t, t + 1) for t in range(times - 1)]
    rightward = [(s, s + 1) for s in range(tiles) if s % ACROSS < ACROSS - 1]
    leftward = [(s, s - 1) for s in range(tiles) if s % ACROSS > 0]
    downward = [(s, s + ACROSS) for s in range(tiles - ACROSS)]
    upward = [(s, s - ACROSS) for s in range(ACROSS, tiles)]

    sums = group_sums(own, tiles)
    past = lax.ppermute(own, "tm", later)
    left = lax.ppermute(own[:, :, -1], "space", rightward)
    right = lax.ppermute(own[:, :, 0], "space", leftward)
    sums = lax.all_to_all(sums, "space", 0, 0).sum(0, keepdims=True)
    last = jnp.concatenate([own[:, -1], left[:, -1:], right[:, -1:]], axis=1)
    start = jnp.concatenate([own[:, 0], left[:, :1], right[:, :1]], axis=1)
    up = lax.ppermute(last, "space", downward)
    down = lax.ppermute(start, "space", upward)
    sums = lax.all_to_all(jnp.broadcast_to(sums, (times, 1, 128)), "tm", 0, 0).reshape(times, 128)
    blank = jnp.zeros((count, 12, channels), BF16)
    edge = jnp.concatenate([left, right, up[:, :width], down[:, :width], up[:, width:], down[:, width:], blank], axis=1)
    past_edge = lax.ppermute(edge, "tm", later)

    taps = conv_filter.reshape(9, 3 * channels, channels)
    output = convolve(place, sums, own, past, edge, past_edge, norm_gain[None], norm_shift[None], taps,
                      conv_offset[None])
    return output[:, None]


def solution(mesh):
    placed = (P("tm", "space", None, None, None), P(), P(), P(), P())
    return jax.shard_map(
        local,
        mesh=mesh,
        in_specs=placed,
        out_specs=P("tm", "space", None, None, None),
        check_vma=False,
    )
```

time: 147 us -> 67.7 us (0.46)
  the two profiles are of different devices: /device:TPU:132 before, /device:TPU:1 now
where the time goes in v1:
time: 67.7 us; the launch traced here: 67.3 us
  starting transfers between devices  40.8 us (60%)
  waiting for transfers between devices  13.8 us (20%)
  Pallas kernels  7.7 us (11%)
  local copies, waits for them, and re-layouts  4.64 us (7%)
    all_to_all x1, starting transfers between devices, local(): sums = lax.all_to_all(sums, 'space', 0, 0).sum(0, keepdims=True)  9.8 us
    all_to_all x1, starting transfers between devices, local(): lax.all_to_all(jnp.broadcast_to(sums, (times, 1, 128)), 'tm', 0, 0)  9.04 us
    all_to_all x1, waiting for transfers between devices, local(): lax.all_to_all(jnp.broadcast_to(sums, (times, 1, 128)), 'tm', 0, 0)  8.18 us
    ppermute x1, starting transfers between devices, local(): up = lax.ppermute(last, 'space', downward)  5.81 us
    pallas_call x1, Pallas kernels, convolve(): pl.pallas_call(conv_kernel, out_shape=jax.ShapeDtypeStruct(own.shape, BF1...  5.73 us
    ppermute x1, starting transfers between devices, local(): left = lax.ppermute(own[:, :, -1], 'space', rightward)  4.84 us
    ppermute x1, starting transfers between devices, local(): past = lax.ppermute(own, 'tm', later)  4.06 us
    ppermute x1, starting transfers between devices, local(): past_edge = lax.ppermute(edge, 'tm', later)  3.5 us
  transfers between devices with their start and end apart: 8, of which 3 were waited for; matrix products, arithmetic and copies ran while one was open for 2% of the time, Pallas kernels for 3%

profile of v1, /device:TPU:1, one launch (start us, length us, event | category | flops | bytes accessed | tf_op | source)
XLA Modules:
  0.0 67.3 jit_solution(5266997064008132280)
XLA Ops:
  0.0 0.0 copy-start
  0.0 0.0 copy-start.3
  0.0 0.0 copy-start.4
  0.0 0.0 copy-start.2
  0.0 1.4 %copy.36 = bf16[2,1,16,32,256]{4,2,0,3,1:T(8,128)(2,1)S(1)} copy(bf16[2,1,16,32,256]{4,3,2,1,0:T(8,128)(2,1)} %param.5) | data formatting | bytes 1048576 | tf_op args[0]
  1.4 4.1 %collective-permute-start = (bf16[2,16,32,256]{3,1,0,2:T(8,128)(2,1)S(1)}, bf16[2,16,32,256]{3,1,0,2:T(8,128)(2,1)S(1)}, u32[]{:S(2)}, u32[]{:S(2)}) collective-permute-start(bf16[2,16,32,256]{3,1,0,2:T(8,128)(2,1)S(1)} %bitcast.31), channel_id=1, source_target_pairs={{0,16},{16,32},{32,48},{48,64},{64,80},{80,96},{96,112},{112,128},... | collective-permute-start | bytes 1572872 | tf_op jit(solution)/shard_map/ppermute | solution.py:175
  5.5 4.8 %collective-permute-start.1 = (bf16[2,16,256]{2,1,0:T(8,128)(2,1)S(1)}, bf16[2,16,256]{2,1,0:T(8,128)(2,1)S(1)}, u32[]{:S(2)}, u32[]{:S(2)}) collective-permute-start(bf16[2,16,256]{2,1,0:T(8,128)(2,1)S(1)} %get-tuple-element.8), channel_id=1, source_target_pairs={{0,1},{1,2},{2,3},{4,5},{5,6},{6,7},{8,9},{9,10},{10,11},{12,13},{... | collective-permute-start | bytes 49160 | tf_op jit(solution)/shard_map/ppermute | solution.py:176
  10.3 2.5 %collective-permute-start.2 = (bf16[2,16,256]{2,1,0:T(8,128)(2,1)S(1)}, bf16[2,16,256]{2,1,0:T(8,128)(2,1)S(1)}, u32[]{:S(2)}, u32[]{:S(2)}) collective-permute-start(bf16[2,16,256]{2,1,0:T(8,128)(2,1)S(1)} %get-tuple-element.7), channel_id=1, source_target_pairs={{1,0},{2,1},{3,2},{5,4},{6,5},{7,6},{9,8},{10,9},{11,10},{13,12},{... | collective-permute-start | bytes 49160 | tf_op jit(solution)/shard_map/ppermute | solution.py:177
  12.8 0.1 fusion
  13.0 0.0 collective-permute-done.1
  13.0 2.4 %collective-permute-done.2 = bf16[2,16,256]{2,1,0:T(8,128)(2,1)S(1)} collective-permute-done((bf16[2,16,256]{2,1,0:T(8,128)(2,1)S(1)}, bf16[2,16,256]{2,1,0:T(8,128)(2,1)S(1)}, u32[]{:S(2)}, u32[]{:S(2)}) %collective-permute-start.2) | collective-permute-done | bytes 16416 | tf_op jit(solution)/shard_map/ppermute | solution.py:177
  15.4 5.8 %collective-permute-start.3 = (bf16[2,34,256]{2,1,0:T(8,128)(2,1)S(1)}, bf16[2,34,256]{2,1,0:T(8,128)(2,1)S(1)}, u32[]{:S(2)}, u32[]{:S(2)}) collective-permute-start(bf16[2,34,256]{2,1,0:T(8,128)(2,1)S(1)} %pad_maximum_fusion), channel_id=1, source_target_pairs={{0,4},{1,5},{2,6},{3,7},{4,8},{5,9},{6,10},{7,11},{8,12},{9,13},{1... | collective-permute-start | bytes 104456 | tf_op jit(solution)/shard_map/ppermute | solution.py:181
  21.3 1.3 %collective-permute-start.4 = (bf16[2,34,256]{2,1,0:T(8,128)(2,1)S(1)}, bf16[2,34,256]{2,1,0:T(8,128)(2,1)S(1)}, u32[]{:S(2)}, u32[]{:S(2)}) collective-permute-start(bf16[2,34,256]{2,1,0:T(8,128)(2,1)S(1)} %pad_maximum_fusion.1), channel_id=1, source_target_pairs={{4,0},{5,1},{6,2},{7,3},{8,4},{9,5},{10,6},{11,7},{12,8},{13,9},{1... | collective-permute-start | bytes 104456 | tf_op jit(solution)/shard_map/ppermute | solution.py:182
  22.6 2.0 %shard_map.55 = f32[16,1,128]{2,1,0:T(1,128)} custom-call(bf16[2,16,32,256]{3,2,1,0:T(8,128)(2,1)} %bitcast.24), custom_call_target="tpu_custom_call" | custom-call | flops 1048576 | bytes 524288 | tf_op jit(solution)/shard_map/pallas_call | solution.py:49
  24.5 9.8 %all-to-all-start = ((f32[16,1,128]{2,1,0:T(1,128)}), f32[16,1,128]{2,1,0:T(1,128)S(1)}, u32[]{:S(2)}, u32[]{:S(2)}) async-start(f32[16,1,128]{2,1,0:T(1,128)} %shard_map.55), calls=%async_computation | async-start | bytes 16384 | tf_op jit(solution)/shard_map/all_to_all | solution.py:178
  34.3 0.0 collective-permute-done.3
  34.4 0.0 collective-permute-done.4
  34.4 0.2 concatenate.11.edge_ref
  34.6 3.5 %collective-permute-start.5 = (bf16[2,112,256]{2,1,0:T(8,128)(2,1)S(1)}, bf16[2,112,256]{2,1,0:T(8,128)(2,1)S(1)}, u32[]{:S(2)}, u32[]{:S(2)}) collective-permute-start(bf16[2,112,256]{2,1,0:T(8,128)(2,1)S(1)} %concatenate.11.edge_ref), channel_id=1, source_target_pairs={{0,16},{16,32},{32,48},{48,64},{64,80},{80,96},{96,112},{112,128},... | collective-permute-start | bytes 344072 | tf_op jit(solution)/shard_map/ppermute | solution.py:186
  38.1 3.2 %all-to-all-done = f32[16,1,128]{2,1,0:T(1,128)S(1)} async-done(((f32[16,1,128]{2,1,0:T(1,128)}), f32[16,1,128]{2,1,0:T(1,128)S(1)}, u32[]{:S(2)}, u32[]{:S(2)}) %all-to-all-start) | async-done | bytes 8224 | tf_op jit(solution)/shard_map/all_to_all | solution.py:178
  41.3 0.6 broadcast_in_dim.21
  41.9 9.0 %all-to-all-start.1 = ((f32[32,1,128]{2,1,0:T(1,128)}), f32[32,1,128]{2,1,0:T(1,128)S(1)}, u32[]{:S(2)}, u32[]{:S(2)}) async-start(f32[32,1,128]{2,1,0:T(1,128)} %broadcast_in_dim.21), calls=%async_computation.1 | async-start | bytes 32768 | tf_op jit(solution)/shard_map/all_to_all | solution.py:183
  51.0 0.1 pad_add_fusion.place_ref
  51.1 0.0 collective-permute-done
  51.1 0.3 copy.30.past_ref
  51.4 8.2 %all-to-all-done.1 = f32[32,1,128]{2,1,0:T(1,128)S(1)} async-done(((f32[32,1,128]{2,1,0:T(1,128)}), f32[32,1,128]{2,1,0:T(1,128)S(1)}, u32[]{:S(2)}, u32[]{:S(2)}) %all-to-all-start.1) | async-done | bytes 16416 | tf_op jit(solution)/shard_map/all_to_all | solution.py:183
  59.5 0.0 collective-permute-done.5.past_edge_ref
  59.5 0.0 copy-done
  59.5 0.0 copy-done.3
  59.5 0.0 copy-done.4
  59.6 0.0 copy-done.2
  59.6 0.0 copy-start.1
  59.6 2.0 %copy-done.1 = bf16[3,3,3,256,256]{4,3,2,1,0:T(8,128)(2,1)S(1)} copy-done((bf16[3,3,3,256,256]{4,3,2,1,0:T(8,128)(2,1)S(1)}, bf16[3,3,3,256,256]{4,3,2,1,0:T(8,128)(2,1)}, u32[]{:S(2)}) %copy-start.1) | copy-done | bytes 3538968
  61.6 5.7 %shard_map.56 = bf16[2,16,32,256]{3,2,1,0:T(8,128)(2,1)} custom-call(s32[3]{0:T(128)S(1)} %pad_add_fusion.place_ref, f32[32,128]{1,0:T(8,128)S(1)} %bitcast.26, bf16[2,16,32,256]{3,2,1,0:T(8,128)(2,1)S(1)} %bitcast.25, bf16[2,16,32,256]{3,2,1,0:T(8,128)(2,1)S(1)} %copy.30.past_ref, bf16[2,112,256]{2,1,0:T(8,128)(2,1)S(1)} %concatenate.11.edge_ref, ...), custom_call_target="tpu_custom_call" | custom-call | flops 4294967296 | bytes 6291456 | tf_op jit(solution)/shard_map/pallas_call | solution.py:149
  (13 shorter events, 0.1 us)
Async XLA Ops:
  0.0 59.5 %copy-start = (bf16[2,1,16,32,256]{4,3,2,1,0:T(8,128)(2,1)S(1)}, bf16[2,1,16,32,256]{4,3,2,1,0:T(8,128)(2,1)}, u32[]{:S(2)}) copy-start(bf16[2,1,16,32,256]{4,3,2,1,0:T(8,128)(2,1)} %param.5) | copy-start | bytes 1572868
  0.0 59.5 %copy-start.3 = (f32[256]{0:T(256)S(1)}, f32[256]{0:T(256)}, u32[]{:S(2)}) copy-start(f32[256]{0:T(256)} %param.7) | copy-start | bytes 3076
  0.0 59.5 %copy-start.4 = (f32[256]{0:T(256)S(1)}, f32[256]{0:T(256)}, u32[]{:S(2)}) copy-start(f32[256]{0:T(256)} %param.9) | copy-start | bytes 3076
  0.0 59.5 %copy-start.2 = (f32[256]{0:T(256)S(1)}, f32[256]{0:T(256)}, u32[]{:S(2)}) copy-start(f32[256]{0:T(256)} %param.6) | copy-start | bytes 3076
  1.4 49.6 %collective-permute-start = (bf16[2,16,32,256]{3,1,0,2:T(8,128)(2,1)S(1)}, bf16[2,16,32,256]{3,1,0,2:T(8,128)(2,1)S(1)}, u32[]{:S(2)}, u32[]{:S(2)}) collective-permute-start(bf16[2,16,32,256]{3,1,0,2:T(8,128)(2,1)S(1)} %bitcast.31), channel_id=1, source_target_pairs={{0,16},{16,32},{32,48},{48,64},{64,80},{80,96},{96,112},{112,128},... | collective-permute-start | bytes 1572872 | tf_op jit(solution)/shard_map/ppermute | solution.py:175
  5.5 7.5 %collective-permute-start.1 = (bf16[2,16,256]{2,1,0:T(8,128)(2,1)S(1)}, bf16[2,16,256]{2,1,0:T(8,128)(2,1)S(1)}, u32[]{:S(2)}, u32[]{:S(2)}) collective-permute-start(bf16[2,16,256]{2,1,0:T(8,128)(2,1)S(1)} %get-tuple-element.8), channel_id=1, source_target_pairs={{0,1},{1,2},{2,3},{4,5},{5,6},{6,7},{8,9},{9,10},{10,11},{12,13},{... | collective-permute-start | bytes 49160 | tf_op jit(solution)/shard_map/ppermute | solution.py:176
  10.3 5.1 %collective-permute-start.2 = (bf16[2,16,256]{2,1,0:T(8,128)(2,1)S(1)}, bf16[2,16,256]{2,1,0:T(8,128)(2,1)S(1)}, u32[]{:S(2)}, u32[]{:S(2)}) collective-permute-start(bf16[2,16,256]{2,1,0:T(8,128)(2,1)S(1)} %get-tuple-element.7), channel_id=1, source_target_pairs={{1,0},{2,1},{3,2},{5,4},{6,5},{7,6},{9,8},{10,9},{11,10},{13,12},{... | collective-permute-start | bytes 49160 | tf_op jit(solution)/shard_map/ppermute | solution.py:177
  15.4 18.9 %collective-permute-start.3 = (bf16[2,34,256]{2,1,0:T(8,128)(2,1)S(1)}, bf16[2,34,256]{2,1,0:T(8,128)(2,1)S(1)}, u32[]{:S(2)}, u32[]{:S(2)}) collective-permute-start(bf16[2,34,256]{2,1,0:T(8,128)(2,1)S(1)} %pad_maximum_fusion), channel_id=1, source_target_pairs={{0,4},{1,5},{2,6},{3,7},{4,8},{5,9},{6,10},{7,11},{8,12},{9,13},{1... | collective-permute-start | bytes 104456 | tf_op jit(solution)/shard_map/ppermute | solution.py:181
  21.3 13.1 %collective-permute-start.4 = (bf16[2,34,256]{2,1,0:T(8,128)(2,1)S(1)}, bf16[2,34,256]{2,1,0:T(8,128)(2,1)S(1)}, u32[]{:S(2)}, u32[]{:S(2)}) collective-permute-start(bf16[2,34,256]{2,1,0:T(8,128)(2,1)S(1)} %pad_maximum_fusion.1), channel_id=1, source_target_pairs={{4,0},{5,1},{6,2},{7,3},{8,4},{9,5},{10,6},{11,7},{12,8},{13,9},{1... | collective-permute-start | bytes 104456 | tf_op jit(solution)/shard_map/ppermute | solution.py:182
  24.5 16.7 %all-to-all-start = ((f32[16,1,128]{2,1,0:T(1,128)}), f32[16,1,128]{2,1,0:T(1,128)S(1)}, u32[]{:S(2)}, u32[]{:S(2)}) async-start(f32[16,1,128]{2,1,0:T(1,128)} %shard_map.55), calls=%async_computation | async-start | bytes 16384 | tf_op jit(solution)/shard_map/all_to_all | solution.py:178
  34.6 25.0 %collective-permute-start.5 = (bf16[2,112,256]{2,1,0:T(8,128)(2,1)S(1)}, bf16[2,112,256]{2,1,0:T(8,128)(2,1)S(1)}, u32[]{:S(2)}, u32[]{:S(2)}) collective-permute-start(bf16[2,112,256]{2,1,0:T(8,128)(2,1)S(1)} %concatenate.11.edge_ref), channel_id=1, source_target_pairs={{0,16},{16,32},{32,48},{48,64},{64,80},{80,96},{96,112},{112,128},... | collective-permute-start | bytes 344072 | tf_op jit(solution)/shard_map/ppermute | solution.py:186
  41.9 17.6 %all-to-all-start.1 = ((f32[32,1,128]{2,1,0:T(1,128)}), f32[32,1,128]{2,1,0:T(1,128)S(1)}, u32[]{:S(2)}, u32[]{:S(2)}) async-start(f32[32,1,128]{2,1,0:T(1,128)} %broadcast_in_dim.21), calls=%async_computation.1 | async-start | bytes 32768 | tf_op jit(solution)/shard_map/all_to_all | solution.py:183
  59.6 2.0 %copy-start.1 = (bf16[3,3,3,256,256]{4,3,2,1,0:T(8,128)(2,1)S(1)}, bf16[3,3,3,256,256]{4,3,2,1,0:T(8,128)(2,1)}, u32[]{:S(2)}) copy-start(bf16[3,3,3,256,256]{4,3,2,1,0:T(8,128)(2,1)} %param.8) | copy-start | bytes 10616836

commit v2 on v1

v2 whole, which is shorter than its diff:
```python
import functools

import jax
import jax.numpy as jnp
from jax import lax
from jax.experimental import pallas as pl
from jax.experimental.pallas import tpu as pltpu
from jax.sharding import PartitionSpec as P

GROUPS = 32
ACROSS = 4
F32, BF16 = jnp.float32, jnp.bfloat16
SMALL = pltpu.CompilerParams(vmem_limit_bytes=8 << 20)
LARGE = pltpu.CompilerParams(vmem_limit_bytes=60 << 20)
VMEM = pl.BlockSpec(memory_space=pltpu.VMEM)
SMEM = pl.BlockSpec(memory_space=pltpu.SMEM)
AWAY = pl.BlockSpec(memory_space=pltpu.HBM)


def in_hbm(array):
    return pltpu.with_memory_space_constraint(array, pltpu.HBM)


def cost(flops):
    return pl.CostEstimate(flops=flops, bytes_accessed=1 << 17, transcendentals=0)


def split(value):
    high = value.astype(BF16)
    rest = value - high.astype(F32)
    middle = rest.astype(BF16)
    low = (rest - middle.astype(F32)).astype(BF16)
    return high, middle, low


def exact_dot(value, table):
    return sum(jnp.dot(part, table, preferred_element_type=F32) for part in split(value))


def split_rows(row):
    high, middle, low = (part.astype(F32) for part in split(row))
    upper = jnp.concatenate([high, middle], axis=1)
    lower = jnp.concatenate([low, jnp.zeros_like(low)], axis=1)
    place = lax.broadcasted_iota(jnp.int32, (16, upper.shape[1]), 0)
    return jnp.where(place == 0, upper, jnp.where(place == 1, lower, 0.0))


def joined_row(block):
    upper, lower = block[0:1], block[1:2]
    return upper[:, :128] + upper[:, 128:] + lower[:, :128]


def sums_kernel(frames_hbm, gain_hbm, shift_hbm, offset_hbm, message_ref, columns_ref, gain_ref, shift_ref,
                offset_ref, arrived, *, frames):
    rows, width, channels = frames_hbm.shape
    height = rows // frames
    per_group = channels // GROUPS
    part = rows // 4
    fetches = []
    for at in range(4):
        span = pl.ds(at * part, part)
        fetches.append(pltpu.make_async_copy(frames_hbm.at[span], message_ref.at[span], arrived.at[at]))
        fetches[-1].start()
    small = ((gain_hbm, gain_ref), (shift_hbm, shift_ref), (offset_hbm, offset_ref))
    for at, (source, target) in enumerate(small):
        fetches.append(pltpu.make_async_copy(source, target, arrived.at[4 + at]))
        fetches[-1].start()
    message_ref[rows:] = jnp.zeros((message_ref.shape[0] - rows, width, channels), BF16)
    channel = lax.broadcasted_iota(jnp.int32, (channels, 128), 0)
    lane = lax.broadcasted_iota(jnp.int32, (channels, 128), 1)
    total = jnp.zeros((8, 128), F32)
    for frame in range(frames):
        plain = jnp.zeros((8, channels), F32)
        square = jnp.zeros((8, channels), F32)
        firsts, lasts = [], []
        for row in range(frame * height, (frame + 1) * height):
            if row % part == 0:
                fetches[row // part].wait()
            block = message_ref[row].astype(F32)
            firsts.append(block[0:1])
            lasts.append(block[width - 1 : width])
            block = block.reshape(width // 8, 8, channels)
            plain = plain + block.sum(0)
            square = square + (block * block).sum(0)
        for kind, value in enumerate((plain, square)):
            slot = (kind * frames + frame) * GROUPS
            table = jnp.where(lane == slot + channel // per_group, 1.0, 0.0).astype(BF16)
            total = total + exact_dot(value, table)
        columns_ref[frame * height : (frame + 1) * height] = jnp.concatenate(firsts, axis=0).astype(BF16)
        columns_ref[rows + frame * height : rows + (frame + 1) * height] = jnp.concatenate(lasts, axis=0).astype(BF16)
    columns_ref[2 * rows : 2 * rows + 16] = split_rows(total.sum(0, keepdims=True)).astype(BF16)
    for fetch in fetches[4:]:
        fetch.wait()


def group_sums(own, gain, shift, offset):
    count, height, width, channels = own.shape
    rows = count * height
    vector = jax.ShapeDtypeStruct(gain.shape, F32)
    return pl.pallas_call(
        functools.partial(sums_kernel, frames=count),
        out_shape=[
            jax.ShapeDtypeStruct((rows + 4 * count, width, channels), BF16),
            jax.ShapeDtypeStruct((2 * rows + 16, channels), BF16),
            vector,
            vector,
            vector,
        ],
        in_specs=[AWAY] * 4,
        out_specs=[VMEM] * 5,
        scratch_shapes=[pltpu.SemaphoreType.DMA((7,))],
        compiler_params=SMALL,
        cost_estimate=cost(1 << 20),
    )(in_hbm(own.reshape(rows, width, channels)), in_hbm(gain), in_hbm(shift), in_hbm(offset))


def beside(index, step, count):
    return jnp.clip(index + step, 0, count - 1)


def rows_kernel(place_ref, message_ref, sides_ref, out_ref, *, frames, height):
    width, channels = message_ref.shape[1:]
    members, receivers = sides_ref.shape[0], out_ref.shape[0]
    rows = frames * height
    row_of, col_of = place_ref[1] // ACROSS, place_ref[1] % ACROSS
    on_left, on_right = beside(col_of, -1, members), beside(col_of, 1, members)
    total = jnp.zeros((1, 128), F32)
    for member in range(members):
        total = total + joined_row(sides_ref[member, 2 * rows : 2 * rows + 16].astype(F32))
    upper = lower = split_rows(total)
    place = lax.broadcasted_iota(jnp.int32, (16, channels), 0)
    for frame in range(frames):
        left = sides_ref[on_left, rows + frame * height : rows + (frame + 1) * height].astype(F32)
        right = sides_ref[on_right, frame * height : (frame + 1) * height].astype(F32)
        for at, side in enumerate((left, right)):
            upper = jnp.where(place == 2 + 2 * frame + at, side[0:1], upper)
            lower = jnp.where(place == 2 + 2 * frame + at, side[height - 1 : height], lower)
    for receiver in range(receivers):
        is_above = receiver < row_of
        for frame in range(frames):
            row = frame * height + jnp.where(is_above, 0, height - 1)
            out_ref[receiver, frame * width : (frame + 1) * width] = message_ref[row]
        ends = jnp.where(is_above, upper, lower)
        out_ref[receiver, frames * width : frames * width + 16] = ends.astype(BF16)


def edge_rows(place, message, sides, frames, height, receivers):
    width, channels = message.shape[1:]
    return pl.pallas_call(
        functools.partial(rows_kernel, frames=frames, height=height),
        out_shape=jax.ShapeDtypeStruct((receivers, frames * width + 16, channels), BF16),
        in_specs=[SMEM, VMEM, VMEM],
        out_specs=VMEM,
        compiler_params=SMALL,
        cost_estimate=cost(1 << 20),
    )(place, message, sides)


def border_kernel(place_ref, message_ref, sides_ref, rows_ref, out_ref, sums_ref, *, frames, height):
    width, channels = message_ref.shape[1:]
    members, across = rows_ref.shape[0], sides_ref.shape[0]
    rows = frames * height
    row_of, col_of = place_ref[1] // ACROSS, place_ref[1] % ACROSS
    on_left, on_right = beside(col_of, -1, across), beside(col_of, 1, across)
    above, below = beside(row_of, -1, members), beside(row_of, 1, members)
    ends_at = frames * width
    total = jnp.zeros((1, 128), F32)
    for member in range(members):
        total = total + joined_row(rows_ref[member, ends_at : ends_at + 16].astype(F32))
    sums_ref[...] = jnp.broadcast_to(total[None], sums_ref.shape)
    upper = rows_ref[above, ends_at : ends_at + 16].astype(F32)
    lower = rows_ref[below, ends_at : ends_at + 16].astype(F32)
    place = lax.broadcasted_iota(jnp.int32, (16, channels), 0)
    for frame in range(frames):
        at = rows + 4 * frame
        out_ref[at, 0:height] = sides_ref[on_left, rows + frame * height : rows + (frame + 1) * height]
        out_ref[at, height : 2 * height] = sides_ref[on_right, frame * height : (frame + 1) * height]
        out_ref[at + 1] = rows_ref[above, frame * width : (frame + 1) * width]
        out_ref[at + 2] = rows_ref[below, frame * width : (frame + 1) * width]
        base = 2 + 2 * frame
        cells = (upper[base : base + 1], lower[base : base + 1], upper[base + 1 : base + 2], lower[base + 1 : base + 2])
        corners = jnp.zeros((16, channels), F32)
        for index, cell in enumerate(cells):
            corners = jnp.where(place == index, cell, corners)
        out_ref[at + 3, 0:16] = corners.astype(BF16)


def add_border(place, message, sides, rows, frames, height, receivers):
    return pl.pallas_call(
        functools.partial(border_kernel, frames=frames, height=height),
        out_shape=[
            jax.ShapeDtypeStruct(message.shape, BF16),
            jax.ShapeDtypeStruct((receivers, 1, 128), F32),
        ],
        in_specs=[SMEM, VMEM, VMEM, VMEM],
        out_specs=[VMEM, VMEM],
        input_output_aliases={1: 0},
        compiler_params=SMALL,
        cost_estimate=cost(1 << 20),
    )(place, message, sides, rows)


def norm_scales(sums, gain, time, cells):
    channels = gain.shape[1]
    per_group = channels // GROUPS
    index = lax.broadcasted_iota(jnp.int32, sums.shape, 0)
    lane = lax.broadcasted_iota(jnp.int32, (1, 128), 1)
    first = jnp.where((lane // GROUPS) % 2 == 0, 1.0, 0.0).astype(F32)
    before = jnp.where(index < time - 1, sums, 0.0).sum(0, keepdims=True)
    past = jnp.where(index == time - 1, sums, 0.0).sum(0, keepdims=True)
    own = jnp.where(index == time, sums, 0.0).sum(0, keepdims=True)
    running = jnp.concatenate(
        [before + past * first, before + past, before + past + own * first, before + past + own]
        + [jnp.zeros((4, 128), F32)],
        axis=0,
    )
    slot = lax.broadcasted_iota(jnp.int32, (128, channels), 0)
    channel = lax.broadcasted_iota(jnp.int32, (128, channels), 1)
    wide = []
    for kind in range(2):
        table = (slot // (2 * GROUPS) == kind) & (slot % GROUPS == channel // per_group)
        wide.append(exact_dot(running, jnp.where(table, 1.0, 0.0).astype(BF16)))
    frame_row = lax.broadcasted_iota(jnp.int32, (8, channels), 0)
    count = jnp.maximum((time * 2 - 1 + frame_row) * cells, 1).astype(F32)
    mean = wide[0] / count
    spread = wide[1] / count - mean * mean
    return mean, lax.rsqrt(spread + 1e-06) * gain


def conv_kernel(place_ref, sums_ref, past_ref, own_ref, gain_ref, shift_ref, offset_ref, filter_hbm, out_ref, shifted,
                taps_ref, arrived):
    fetch = pltpu.make_async_copy(filter_hbm, taps_ref, arrived)
    fetch.start()
    frames, height, width, channels = out_ref.shape
    rows = frames * height
    time, tile, tiles = place_ref[0], place_ref[1], place_ref[2]
    row_of, col_of = tile // ACROSS, tile % ACROSS
    down_max = tiles // ACROSS - 1
    mean, scale = norm_scales(sums_ref[...], gain_ref[...], time, height * width * tiles * (channels // GROUPS))
    shift = shift_ref[...]

    def activate(value, which):
        u = (value.astype(F32) - mean[which : which + 1]) * scale[which : which + 1] + shift
        return u / (1.0 + jnp.exp(-u))

    has_left = jnp.where(col_of > 0, 1.0, 0.0).astype(F32)
    has_right = jnp.where(col_of < ACROSS - 1, 1.0, 0.0).astype(F32)
    has_up = jnp.where(row_of > 0, 1.0, 0.0).astype(F32)
    has_down = jnp.where(row_of < down_max, 1.0, 0.0).astype(F32)
    has_past = jnp.where(time > 0, 1.0, 0.0).astype(F32)
    place = lax.broadcasted_iota(jnp.int32, (width, channels), 0)

    def put(which, row, center, left, right):
        at = pl.ds((which * (height + 2) + row) * width, width)
        toward = jnp.where(place == 0, left, pltpu.roll(center, 1, 0))
        away = jnp.where(place == width - 1, right, pltpu.roll(center, width - 1, 0))
        shifted[at, 0:channels] = toward.astype(BF16)
        shifted[at, channels : 2 * channels] = center.astype(BF16)
        shifted[at, 2 * channels : 3 * channels] = away.astype(BF16)

    def prepare(which):
        source = past_ref if which < 2 else own_ref
        here = has_past if which < 2 else jnp.ones((), F32)
        frame = which % 2
        at = rows + 4 * frame
        left = activate(source[at, 0:height], which) * (has_left * here)
        right = activate(source[at, height : 2 * height], which) * (has_right * here)
        up = activate(source[at + 1], which) * (has_up * here)
        down = activate(source[at + 2], which) * (has_down * here)
        corners = activate(source[at + 3, 0:16], which) * here
        put(which, 0, up, corners[0:1] * (has_up * has_left), corners[2:3] * (has_up * has_right))
        put(which, height + 1, down, corners[1:2] * (has_down * has_left), corners[3:4] * (has_down * has_right))
        for row in range(height):
            center = activate(source[frame * height + row], which)
            if which < 2:
                center = center * here
            put(which, row + 1, center, left[row : row + 1], right[row : row + 1])

    for which in range(4):
        prepare(which)
    fetch.wait()
    for frame in range(frames):
        total = jnp.zeros((height * width, channels), F32)
        for lagged in range(3):
            for vertical in range(3):
                at = ((frame + lagged) * (height + 2) + vertical) * width
                total = total + jnp.dot(
                    shifted[at : at + height * width, :],
                    taps_ref[lagged * 3 + vertical],
                    preferred_element_type=F32,
                )
        value = own_ref[frame * height : (frame + 1) * height].astype(F32).reshape(height * width, channels)
        value = value + (total + offset_ref[...])
        out_ref[frame] = value.astype(BF16).reshape(height, width, channels)


def convolve(place, sums, past, own, gain, shift, offset, taps, shape):
    frames, height, width, channels = shape
    return pl.pallas_call(
        conv_kernel,
        out_shape=jax.ShapeDtypeStruct(shape, BF16),
        in_specs=[SMEM, VMEM, VMEM, VMEM, VMEM, VMEM, VMEM, AWAY],
        out_specs=VMEM,
        scratch_shapes=[
            pltpu.VMEM((4 * (height + 2) * width, 3 * channels), BF16),
            pltpu.VMEM(taps.shape, BF16),
            pltpu.SemaphoreType.DMA(()),
        ],
        compiler_params=pltpu.CompilerParams(vmem_limit_bytes=32 << 20),
        cost_estimate=pl.CostEstimate(flops=4 << 30, bytes_accessed=6 << 20, transcendentals=1 << 20),
    )(place, sums, past, own, gain, shift, offset, in_hbm(taps))


def local(frames, norm_gain, norm_shift, conv_filter, conv_offset):
    own = frames[:, 0]
    count, height, width, channels = own.shape
    times, tiles = lax.axis_size("tm"), lax.axis_size("space")
    place = jnp.stack([lax.axis_index("tm"), lax.axis_index("space"), jnp.int32(tiles)]).astype(jnp.int32)

    later = [(t, t + 1) for t in range(times - 1)]
    across = [[row + col for col in range(ACROSS)] for row in range(0, tiles, ACROSS)]
    along = [[row + col for row in range(0, tiles, ACROSS)] for col in range(ACROSS)]

    message, columns, gain, shift, offset = group_sums(own, norm_gain[None], norm_shift[None], conv_offset[None])
    sides = lax.all_gather(columns, "space", axis_index_groups=across)
    rows = edge_rows(place, message, sides, count, height, tiles // ACROSS)
    rows = lax.all_to_all(rows, "space", 0, 0, axis_index_groups=along)
    message, sums = add_border(place, message, sides, rows, count, height, times)
    past = lax.ppermute(message, "tm", later)
    sums = lax.all_to_all(sums, "tm", 0, 0).reshape(times, 128)

    taps = conv_filter.reshape(9, 3 * channels, channels)
    output = convolve(place, sums, past, message, gain, shift, offset, taps, own.shape)
    return output[:, None]


def solution(mesh):
    placed = (P("tm", "space", None, None, None), P(), P(), P(), P())
    return jax.shard_map(
        local,
        mesh=mesh,
        in_specs=placed,
        out_specs=P("tm", "space", None, None, None),
        check_vma=False,
    )
```

time: 67.7 us -> 58.6 us (0.87)
  the two profiles are of different devices: /device:TPU:1 before, /device:TPU:64 now
where the time goes in v2:
time: 58.6 us; the launch traced here: 58.4 us
  blocking collectives  44.9 us (77%)
  Pallas kernels  9.86 us (17%)
  starting transfers between devices  3.52 us (6%)
    all_to_all x1, blocking collectives, local(): sums = lax.all_to_all(sums, 'tm', 0, 0).reshape(times, 128)  20.7 us
    all_to_all x1, blocking collectives, local(): rows = lax.all_to_all(rows, 'space', 0, 0, axis_index_groups=along)  15.4 us
    all_gather x1, blocking collectives, local(): sides = lax.all_gather(columns, 'space', axis_index_groups=across)  8.75 us
    pallas_call x1, Pallas kernels, convolve(): pl.pallas_call(conv_kernel, out_shape=jax.ShapeDtypeStruct(shape, BF16),...  7.2 us
    ppermute x1, starting transfers between devices, local(): past = lax.ppermute(message, 'tm', later)  3.52 us
    pallas_call x1, Pallas kernels, group_sums(): pl.pallas_call(functools.partial(sums_kernel, frames=count), out_shape=[j...  1.52 us
  transfers between devices with their start and end apart: 1, of which 0 were waited for; matrix products, arithmetic and copies ran while one was open for 0% of the time, Pallas kernels for 0%

profile of v2, /device:TPU:64, one launch (start us, length us, event | category | flops | bytes accessed | tf_op | source)
XLA Modules:
  0.0 58.4 jit_solution(7477281259504713436)
XLA Ops:
  0.0 1.5 %shard_map.55 = (bf16[40,32,256]{2,1,0:T(8,128)(2,1)S(1)}, bf16[80,256]{1,0:T(8,128)(2,1)S(1)}, f32[1,256]{1,0:T(1,128)S(1)}, f32[1,256]{1,0:T(1,128)S(1)}, f32[1,256]{1,0:T(1,128)S(1)}) custom-call(bf16[32,32,256]{2,1,0:T(8,128)(2,1)} %bitcast.15, f32[1,256]{1,0:T(1,128)} %bitcast.16, f32[1,256]{1,0:T(1,128)} %bitcast.17, f32[1,256]{1,0:T(1,128)} %bitcast.18), custom_call_target="tpu_custom_call" | custom-call | flops 1048576 | bytes 131072 | tf_op jit(solution)/shard_map/pallas_call | solution.py:100
  1.5 8.7 %all-gather = bf16[320,256]{1,0:T(8,128)(2,1)S(1)} all-gather(bf16[80,256]{1,0:T(8,128)(2,1)S(1)} %get-tuple-element.13), channel_id=2, replica_groups={{0,1,2,3},{4,5,6,7},{8,9,10,11},{12,13,14,15},{16,17,18,19},{20,21,22,2..., dimensions={0}, use_global_device_ids=true | all-gather | bytes 204800 | tf_op jit(solution)/shard_map/all_gather | solution.py:325
  10.3 0.1 pad_add_fusion.place_ref
  10.4 0.6 shard_map.56
  10.9 15.4 %all_to_all.10.rows_ref = bf16[4,80,256]{2,1,0:T(8,128)(2,1)S(1)} all-to-all(bf16[4,80,256]{2,1,0:T(8,128)(2,1)S(1)} %shard_map.56), channel_id=1, replica_groups={{0,4,8,12},{1,5,9,13},{2,6,10,14},{3,7,11,15},{16,20,24,28},{17,21,25,2..., dimensions={0} | all-to-all | bytes 327680 | tf_op jit(solution)/shard_map/all_to_all | solution.py:327
  26.3 0.6 shard_map.57
  26.9 3.5 %collective-permute-start = (bf16[40,32,256]{2,1,0:T(8,128)(2,1)S(1)}, bf16[40,32,256]{2,1,0:T(8,128)(2,1)S(1)}, u32[]{:S(2)}, u32[]{:S(2)}) collective-permute-start(bf16[40,32,256]{2,1,0:T(8,128)(2,1)S(1)} %get-tuple-element.15.own_ref), channel_id=1, source_target_pairs={{0,16},{16,32},{32,48},{48,64},{64,80},{80,96},{96,112},{112,128},... | collective-permute-start | bytes 1966088 | tf_op jit(solution)/shard_map/ppermute | solution.py:329
  30.4 20.7 %all_to_all.11 = f32[32,1,128]{2,1,0:T(1,128)S(1)} all-to-all(f32[32,1,128]{2,1,0:T(1,128)S(1)} %get-tuple-element.14), channel_id=1, replica_groups=mesh['tm'=32,'space'=16] {'tm'}, dimensions={0} | all-to-all | bytes 32768 | tf_op jit(solution)/shard_map/all_to_all | solution.py:330
  51.2 0.0 collective-permute-done.past_ref
  51.2 7.2 %shard_map.58 = bf16[2,16,32,256]{3,2,1,0:T(8,128)(2,1)} custom-call(s32[3]{0:T(128)S(1)} %pad_add_fusion.place_ref, f32[32,128]{1,0:T(8,128)S(1)} %bitcast.14, bf16[40,32,256]{2,1,0:T(8,128)(2,1)S(1)} %collective-permute-done.past_ref, bf16[40,32,256]{2,1,0:T(8,128)(2,1)S(1)} %get-tuple-element.15.own_ref, f32[1,256]{1,0:T(1,128)S(1)} %get-tuple-element.16.gain_ref, ...), custom_call_target="tpu_custom_call" | custom-call | flops 4294967296 | bytes 6291456 | tf_op jit(solution)/shard_map/pallas_call | solution.py:299
Async XLA Ops:
  26.9 24.3 %collective-permute-start = (bf16[40,32,256]{2,1,0:T(8,128)(2,1)S(1)}, bf16[40,32,256]{2,1,0:T(8,128)(2,1)S(1)}, u32[]{:S(2)}, u32[]{:S(2)}) collective-permute-start(bf16[40,32,256]{2,1,0:T(8,128)(2,1)S(1)} %get-tuple-element.15.own_ref), channel_id=1, source_target_pairs={{0,16},{16,32},{32,48},{48,64},{64,80},{80,96},{96,112},{112,128},... | collective-permute-start | bytes 1966088 | tf_op jit(solution)/shard_map/ppermute | solution.py:329

commit v3 on v2

--- a/solution.py
+++ b/solution.py
@@ -11,10 +11,12 @@
 ACROSS = 4
 F32, BF16 = jnp.float32, jnp.bfloat16
 SMALL = pltpu.CompilerParams(vmem_limit_bytes=8 << 20)
-LARGE = pltpu.CompilerParams(vmem_limit_bytes=60 << 20)
 VMEM = pl.BlockSpec(memory_space=pltpu.VMEM)
-SMEM = pl.BlockSpec(memory_space=pltpu.SMEM)
 AWAY = pl.BlockSpec(memory_space=pltpu.HBM)
+
+
+def in_vmem(array):
+    return pltpu.with_memory_space_constraint(array, pltpu.VMEM)
 
 
 def in_hbm(array):
@@ -118,11 +120,12 @@
     return jnp.clip(index + step, 0, count - 1)
 
 
-def rows_kernel(place_ref, message_ref, sides_ref, out_ref, *, frames, height):
+def rows_kernel(message_ref, sides_ref, taps_hbm, out_ref, *, frames, height):
     width, channels = message_ref.shape[1:]
     members, receivers = sides_ref.shape[0], out_ref.shape[0]
     rows = frames * height
-    row_of, col_of = place_ref[1] // ACROSS, place_ref[1] % ACROSS
+    tile = lax.axis_index("space")
+    row_of, col_of = tile // ACROSS, tile % ACROSS
     on_left, on_right = beside(col_of, -1, members), beside(col_of, 1, members)
     total = jnp.zeros((1, 128), F32)
     for member in range(members):
@@ -144,23 +147,24 @@
         out_ref[receiver, frames * width : frames * width + 16] = ends.astype(BF16)
 
 
-def edge_rows(place, message, sides, frames, height, receivers):
+def edge_rows(message, sides, taps, frames, height, receivers):
     width, channels = message.shape[1:]
     return pl.pallas_call(
         functools.partial(rows_kernel, frames=frames, height=height),
         out_shape=jax.ShapeDtypeStruct((receivers, frames * width + 16, channels), BF16),
-        in_specs=[SMEM, VMEM, VMEM],
+        in_specs=[VMEM, VMEM, AWAY],
         out_specs=VMEM,
         compiler_params=SMALL,
         cost_estimate=cost(1 << 20),
-    )(place, message, sides)
-
-
-def border_kernel(place_ref, message_ref, sides_ref, rows_ref, out_ref, sums_ref, *, frames, height):
+    )(message, sides, in_hbm(taps))
+
+
+def border_kernel(message_ref, sides_ref, rows_ref, out_ref, sums_ref, *, frames, height):
     width, channels = message_ref.shape[1:]
     members, across = rows_ref.shape[0], sides_ref.shape[0]
     rows = frames * height
-    row_of, col_of = place_ref[1] // ACROSS, place_ref[1] % ACROSS
+    tile = lax.axis_index("space")
+    row_of, col_of = tile // ACROSS, tile % ACROSS
     on_left, on_right = beside(col_of, -1, across), beside(col_of, 1, across)
     above, below = beside(row_of, -1, members), beside(row_of, 1, members)
     ends_at = frames * width
@@ -185,19 +189,19 @@
         out_ref[at + 3, 0:16] = corners.astype(BF16)
 
 
-def add_border(place, message, sides, rows, frames, height, receivers):
+def add_border(message, sides, rows, frames, height, receivers):
     return pl.pallas_call(
         functools.partial(border_kernel, frames=frames, height=height),
         out_shape=[
             jax.ShapeDtypeStruct(message.shape, BF16),
             jax.ShapeDtypeStruct((receivers, 1, 128), F32),
         ],
-        in_specs=[SMEM, VMEM, VMEM, VMEM],
+        in_specs=[VMEM, VMEM, VMEM],
         out_specs=[VMEM, VMEM],
-        input_output_aliases={1: 0},
+        input_output_aliases={0: 0},
         compiler_params=SMALL,
         cost_estimate=cost(1 << 20),
-    )(place, message, sides, rows)
+    )(message, sides, rows)
 
 
 def norm_scales(sums, gain, time, cells):
@@ -227,13 +231,10 @@
     return mean, lax.rsqrt(spread + 1e-06) * gain
 
 
-def conv_kernel(place_ref, sums_ref, past_ref, own_ref, gain_ref, shift_ref, offset_ref, filter_hbm, out_ref, shifted,
-                taps_ref, arrived):
-    fetch = pltpu.make_async_copy(filter_hbm, taps_ref, arrived)
-    fetch.start()
+def conv_kernel(sums_ref, past_ref, own_ref, gain_ref, shift_ref, offset_ref, taps_ref, out_ref, shifted):
     frames, height, width, channels = out_ref.shape
     rows = frames * height
-    time, tile, tiles = place_ref[0], place_ref[1], place_ref[2]
+    time, tile, tiles = lax.axis_index("tm"), lax.axis_index("space"), lax.axis_size("space")
     row_of, col_of = tile // ACROSS, tile % ACROSS
     down_max = tiles // ACROSS - 1
     mean, scale = norm_scales(sums_ref[...], gain_ref[...], time, height * width * tiles * (channels // GROUPS))
@@ -278,7 +279,6 @@
 
     for which in range(4):
         prepare(which)
-    fetch.wait()
     for frame in range(frames):
         total = jnp.zeros((height * width, channels), F32)
         for lagged in range(3):
@@ -294,28 +294,25 @@
         out_ref[frame] = value.astype(BF16).reshape(height, width, channels)
 
 
-def convolve(place, sums, past, own, gain, shift, offset, taps, shape):
+def convolve(sums, past, own, gain, shift, offset, taps, shape):
     frames, height, width, channels = shape
     return pl.pallas_call(
         conv_kernel,
         out_shape=jax.ShapeDtypeStruct(shape, BF16),
-        in_specs=[SMEM, VMEM, VMEM, VMEM, VMEM, VMEM, VMEM, AWAY],
+        in_specs=[VMEM] * 7,
         out_specs=VMEM,
         scratch_shapes=[
             pltpu.VMEM((4 * (height + 2) * width, 3 * channels), BF16),
-            pltpu.VMEM(taps.shape, BF16),
-            pltpu.SemaphoreType.DMA(()),
         ],
         compiler_params=pltpu.CompilerParams(vmem_limit_bytes=32 << 20),
         cost_estimate=pl.CostEstimate(flops=4 << 30, bytes_accessed=6 << 20, transcendentals=1 << 20),
-    )(place, sums, past, own, gain, shift, offset, in_hbm(taps))
+    )(sums, past, own, gain, shift, offset, in_vmem(taps))
 
 
 def local(frames, norm_gain, norm_shift, conv_filter, conv_offset):
     own = frames[:, 0]
     count, height, width, channels = own.shape
     times, tiles = lax.axis_size("tm"), lax.axis_size("space")
-    place = jnp.stack([lax.axis_index("tm"), lax.axis_index("space"), jnp.int32(tiles)]).astype(jnp.int32)
 
     later = [(t, t + 1) for t in range(times - 1)]
     across = [[row + col for col in range(ACROSS)] for row in range(0, tiles, ACROSS)]
@@ -323,14 +320,15 @@
 
     message, columns, gain, shift, offset = group_sums(own, norm_gain[None], norm_shift[None], conv_offset[None])
     sides = lax.all_gather(columns, "space", axis_index_groups=across)
-    rows = edge_rows(place, message, sides, count, height, tiles // ACROSS)
+    taps = conv_filter.reshape(9, 3 * channels, channels)
+    rows = edge_rows(message, sides, taps, count, height, tiles // ACROSS)
     rows = lax.all_to_all(rows, "space", 0, 0, axis_index_groups=along)
-    message, sums = add_border(place, message, sides, rows, count, height, times)
+    message, sums = add_border(message, sides, rows, count, height, times)
     past = lax.ppermute(message, "tm", later)
     sums = lax.all_to_all(sums, "tm", 0, 0).reshape(times, 128)
 
     taps = conv_filter.reshape(9, 3 * channels, channels)
-    output = convolve(place, sums, past, message, gain, shift, offset, taps, own.shape)
+    output = convolve(sums, past, message, gain, shift, offset, taps, own.shape)
     return output[:, None]
 
 

time: 58.6 us -> 55.6 us (0.949)
  Pallas kernels: 9.86 us -> 6.93 us
    pallas_call x1, Pallas kernels: 7.2 us -> 5.2 us  [convolve(): pl.pallas_call(conv_kernel, out_shape=jax.ShapeDtypeStruct(shape, BF16),...]
where the time goes in v3:
time: 55.6 us; the launch traced here: 55.4 us
  blocking collectives  44.9 us (81%)
  Pallas kernels  6.93 us (12%)
  starting transfers between devices  3.52 us (6%)
    all_to_all x1, blocking collectives, local(): sums = lax.all_to_all(sums, 'tm', 0, 0).reshape(times, 128)  20.7 us
    all_to_all x1, blocking collectives, local(): rows = lax.all_to_all(rows, 'space', 0, 0, axis_index_groups=along)  15.4 us
    all_gather x1, blocking collectives, local(): sides = lax.all_gather(columns, 'space', axis_index_groups=across)  8.75 us
    pallas_call x1, Pallas kernels, convolve(): pl.pallas_call(conv_kernel, out_shape=jax.ShapeDtypeStruct(shape, BF16),...  5.2 us
    ppermute x1, starting transfers between devices, local(): past = lax.ppermute(message, 'tm', later)  3.52 us
    pallas_call x1, Pallas kernels, group_sums(): pl.pallas_call(functools.partial(sums_kernel, frames=count), out_shape=[j...  1.67 us
  transfers between devices with their start and end apart: 1, of which 0 were waited for; matrix products, arithmetic and copies ran while one was open for 0% of the time, Pallas kernels for 0%

profile of v3, /device:TPU:64, one launch (start us, length us, event | category | flops | bytes accessed | tf_op | source)
XLA Modules:
  0.0 55.4 jit_solution(3317022943182069968)
XLA Ops:
  0.0 0.0 copy-start
  0.0 1.7 %shard_map.55 = (bf16[40,32,256]{2,1,0:T(8,128)(2,1)S(1)}, bf16[80,256]{1,0:T(8,128)(2,1)S(1)}, f32[1,256]{1,0:T(1,128)S(1)}, f32[1,256]{1,0:T(1,128)S(1)}, f32[1,256]{1,0:T(1,128)S(1)}) custom-call(bf16[32,32,256]{2,1,0:T(8,128)(2,1)} %bitcast.15, f32[1,256]{1,0:T(1,128)} %bitcast.16, f32[1,256]{1,0:T(1,128)} %bitcast.17, f32[1,256]{1,0:T(1,128)} %bitcast.18), custom_call_target="tpu_custom_call" | custom-call | flops 1048576 | bytes 131072 | tf_op jit(solution)/shard_map/pallas_call | solution.py:102
  1.7 8.7 %all-gather = bf16[320,256]{1,0:T(8,128)(2,1)S(1)} all-gather(bf16[80,256]{1,0:T(8,128)(2,1)S(1)} %get-tuple-element.13), channel_id=2, replica_groups={{0,1,2,3},{4,5,6,7},{8,9,10,11},{12,13,14,15},{16,17,18,19},{20,21,22,2..., dimensions={0}, use_global_device_ids=true | all-gather | bytes 204800 | tf_op jit(solution)/shard_map/all_gather | solution.py:322
  10.5 15.4 %all_to_all.10.rows_ref = bf16[4,80,256]{2,1,0:T(8,128)(2,1)S(1)} all-to-all(bf16[4,80,256]{2,1,0:T(8,128)(2,1)S(1)} %shard_map.56), channel_id=1, replica_groups={{0,4,8,12},{1,5,9,13},{2,6,10,14},{3,7,11,15},{16,20,24,28},{17,21,25,2..., dimensions={0} | all-to-all | bytes 327680 | tf_op jit(solution)/shard_map/all_to_all | solution.py:325
  25.9 3.5 %collective-permute-start = (bf16[40,32,256]{2,1,0:T(8,128)(2,1)S(1)}, bf16[40,32,256]{2,1,0:T(8,128)(2,1)S(1)}, u32[]{:S(2)}, u32[]{:S(2)}) collective-permute-start(bf16[40,32,256]{2,1,0:T(8,128)(2,1)S(1)} %get-tuple-element.15.own_ref), channel_id=1, source_target_pairs={{0,16},{16,32},{32,48},{48,64},{64,80},{80,96},{96,112},{112,128},... | collective-permute-start | bytes 1966088 | tf_op jit(solution)/shard_map/ppermute | solution.py:327
  29.4 20.7 %all_to_all.11 = f32[32,1,128]{2,1,0:T(1,128)S(1)} all-to-all(f32[32,1,128]{2,1,0:T(1,128)S(1)} %get-tuple-element.14), channel_id=1, replica_groups=mesh['tm'=32,'space'=16] {'tm'}, dimensions={0} | all-to-all | bytes 32768 | tf_op jit(solution)/shard_map/all_to_all | solution.py:328
  50.2 0.0 collective-permute-done.past_ref
  50.2 0.0 copy-done
  50.2 5.2 %shard_map.58 = bf16[2,16,32,256]{3,2,1,0:T(8,128)(2,1)} custom-call(f32[32,128]{1,0:T(8,128)S(1)} %bitcast.14, bf16[40,32,256]{2,1,0:T(8,128)(2,1)S(1)} %collective-permute-done.past_ref, bf16[40,32,256]{2,1,0:T(8,128)(2,1)S(1)} %get-tuple-element.15.own_ref, f32[1,256]{1,0:T(1,128)S(1)} %get-tuple-element.16.gain_ref, ...), custom_call_target="tpu_custom_call" | custom-call | flops 4294967296 | bytes 6291456 | tf_op jit(solution)/shard_map/pallas_call | solution.py:299
  (2 shorter events, 0.1 us)
Async XLA Ops:
  0.0 50.2 %copy-start = (bf16[3,3,3,256,256]{4,3,2,1,0:T(8,128)(2,1)S(1)}, bf16[3,3,3,256,256]{4,3,2,1,0:T(8,128)(2,1)}, u32[]{:S(2)}) copy-start(bf16[3,3,3,256,256]{4,3,2,1,0:T(8,128)(2,1)} %param.8) | copy-start | bytes 10616836
  25.9 24.3 %collective-permute-start = (bf16[40,32,256]{2,1,0:T(8,128)(2,1)S(1)}, bf16[40,32,256]{2,1,0:T(8,128)(2,1)S(1)}, u32[]{:S(2)}, u32[]{:S(2)}) collective-permute-start(bf16[40,32,256]{2,1,0:T(8,128)(2,1)S(1)} %get-tuple-element.15.own_ref), channel_id=1, source_target_pairs={{0,16},{16,32},{32,48},{48,64},{64,80},{80,96},{96,112},{112,128},... | collective-permute-start | bytes 1966088 | tf_op jit(solution)/shard_map/ppermute | solution.py:327

commit v4 on v3

--- a/solution.py
+++ b/solution.py
@@ -36,7 +36,9 @@
 
 
 def exact_dot(value, table):
-    return sum(jnp.dot(part, table, preferred_element_type=F32) for part in split(value))
+    parts = jnp.concatenate([part.astype(F32) for part in split(value)] + [jnp.zeros_like(value)], axis=0)
+    product = jnp.dot(parts.astype(BF16), table.astype(BF16), preferred_element_type=F32)
+    return product[0:8] + (product[8:16] + product[16:24])
 
 
 def split_rows(row):
@@ -68,9 +70,11 @@
         fetches.append(pltpu.make_async_copy(source, target, arrived.at[4 + at]))
         fetches[-1].start()
     message_ref[rows:] = jnp.zeros((message_ref.shape[0] - rows, width, channels), BF16)
-    channel = lax.broadcasted_iota(jnp.int32, (channels, 128), 0)
-    lane = lax.broadcasted_iota(jnp.int32, (channels, 128), 1)
-    total = jnp.zeros((8, 128), F32)
+    kinds = 2 * frames
+    source = lax.broadcasted_iota(jnp.int32, (kinds * channels, 128), 0)
+    lane = lax.broadcasted_iota(jnp.int32, (kinds * channels, 128), 1)
+    table = jnp.where(lane == source // per_group, 1.0, 0.0)
+    plains, squares = [], []
     for frame in range(frames):
         plain = jnp.zeros((8, channels), F32)
         square = jnp.zeros((8, channels), F32)
@@ -84,12 +88,11 @@
             block = block.reshape(width // 8, 8, channels)
             plain = plain + block.sum(0)
             square = square + (block * block).sum(0)
-        for kind, value in enumerate((plain, square)):
-            slot = (kind * frames + frame) * GROUPS
-            table = jnp.where(lane == slot + channel // per_group, 1.0, 0.0).astype(BF16)
-            total = total + exact_dot(value, table)
+        plains.append(plain)
+        squares.append(square)
         columns_ref[frame * height : (frame + 1) * height] = jnp.concatenate(firsts, axis=0).astype(BF16)
         columns_ref[rows + frame * height : rows + (frame + 1) * height] = jnp.concatenate(lasts, axis=0).astype(BF16)
+    total = exact_dot(jnp.concatenate(plains + squares, axis=1), table)
     columns_ref[2 * rows : 2 * rows + 16] = split_rows(total.sum(0, keepdims=True)).astype(BF16)
     for fetch in fetches[4:]:
         fetch.wait()
@@ -102,7 +105,7 @@
     return pl.pallas_call(
         functools.partial(sums_kernel, frames=count),
         out_shape=[
-            jax.ShapeDtypeStruct((rows + 4 * count, width, channels), BF16),
+            jax.ShapeDtypeStruct((rows + 3 * count + 1, width, channels), BF16),
             jax.ShapeDtypeStruct((2 * rows + 16, channels), BF16),
             vector,
             vector,
@@ -175,18 +178,18 @@
     upper = rows_ref[above, ends_at : ends_at + 16].astype(F32)
     lower = rows_ref[below, ends_at : ends_at + 16].astype(F32)
     place = lax.broadcasted_iota(jnp.int32, (16, channels), 0)
+    corners = jnp.zeros((16, channels), F32)
     for frame in range(frames):
-        at = rows + 4 * frame
+        at = rows + 3 * frame
         out_ref[at, 0:height] = sides_ref[on_left, rows + frame * height : rows + (frame + 1) * height]
         out_ref[at, height : 2 * height] = sides_ref[on_right, frame * height : (frame + 1) * height]
         out_ref[at + 1] = rows_ref[above, frame * width : (frame + 1) * width]
         out_ref[at + 2] = rows_ref[below, frame * width : (frame + 1) * width]
         base = 2 + 2 * frame
         cells = (upper[base : base + 1], lower[base : base + 1], upper[base + 1 : base + 2], lower[base + 1 : base + 2])
-        corners = jnp.zeros((16, channels), F32)
         for index, cell in enumerate(cells):
-            corners = jnp.where(place == index, cell, corners)
-        out_ref[at + 3, 0:16] = corners.astype(BF16)
+            corners = jnp.where(place == 4 * frame + index, cell, corners)
+    out_ref[rows + 3 * frames, 0:16] = corners.astype(BF16)
 
 
 def add_border(message, sides, rows, frames, height, receivers):
@@ -218,20 +221,19 @@
         + [jnp.zeros((4, 128), F32)],
         axis=0,
     )
-    slot = lax.broadcasted_iota(jnp.int32, (128, channels), 0)
-    channel = lax.broadcasted_iota(jnp.int32, (128, channels), 1)
-    wide = []
-    for kind in range(2):
-        table = (slot // (2 * GROUPS) == kind) & (slot % GROUPS == channel // per_group)
-        wide.append(exact_dot(running, jnp.where(table, 1.0, 0.0).astype(BF16)))
+    slot = lax.broadcasted_iota(jnp.int32, (128, 2 * channels), 0)
+    target = lax.broadcasted_iota(jnp.int32, (128, 2 * channels), 1)
+    table = (slot // (2 * GROUPS) == target // channels) & (slot % GROUPS == target % channels // per_group)
+    wide = exact_dot(running, jnp.where(table, 1.0, 0.0))
     frame_row = lax.broadcasted_iota(jnp.int32, (8, channels), 0)
     count = jnp.maximum((time * 2 - 1 + frame_row) * cells, 1).astype(F32)
-    mean = wide[0] / count
-    spread = wide[1] / count - mean * mean
+    mean = wide[:, :channels] / count
+    spread = wide[:, channels:] / count - mean * mean
     return mean, lax.rsqrt(spread + 1e-06) * gain
 
 
-def conv_kernel(sums_ref, past_ref, own_ref, gain_ref, shift_ref, offset_ref, taps_ref, out_ref, shifted):
+def conv_kernel(sums_ref, past_ref, own_ref, gain_ref, shift_ref, offset_ref, taps_ref, out_hbm, shifted,
+                out_ref, sent):
     frames, height, width, channels = out_ref.shape
     rows = frames * height
     time, tile, tiles = lax.axis_index("tm"), lax.axis_index("space"), lax.axis_size("space")
@@ -263,12 +265,13 @@
         source = past_ref if which < 2 else own_ref
         here = has_past if which < 2 else jnp.ones((), F32)
         frame = which % 2
-        at = rows + 4 * frame
+        at = rows + 3 * frame
         left = activate(source[at, 0:height], which) * (has_left * here)
         right = activate(source[at, height : 2 * height], which) * (has_right * here)
         up = activate(source[at + 1], which) * (has_up * here)
         down = activate(source[at + 2], which) * (has_down * here)
-        corners = activate(source[at + 3, 0:16], which) * here
+        corners = activate(source[rows + 3 * frames, 0:16], which) * here
+        corners = corners[4 * frame : 4 * frame + 4]
         put(which, 0, up, corners[0:1] * (has_up * has_left), corners[2:3] * (has_up * has_right))
         put(which, height + 1, down, corners[1:2] * (has_down * has_left), corners[3:4] * (has_down * has_right))
         for row in range(height):
@@ -277,32 +280,54 @@
                 center = center * here
             put(which, row + 1, center, left[row : row + 1], right[row : row + 1])
 
+    pieces = 4
+    size = height * width // pieces
+    totals = {}
+    sends = []
+
+    def gather(which):
+        for frame in range(frames):
+            lagged = which - frame
+            if not 0 <= lagged < 3:
+                continue
+            for piece in range(pieces):
+                for vertical in range(3):
+                    at = (which * (height + 2) + vertical) * width + piece * size
+                    part = jnp.dot(
+                        shifted[at : at + size, :], taps_ref[lagged * 3 + vertical], preferred_element_type=F32
+                    )
+                    totals[frame, piece] = totals[frame, piece] + part if (frame, piece) in totals else part
+                if lagged == 2:
+                    finish(frame, piece)
+
+    def finish(frame, piece):
+        span = height // pieces
+        value = own_ref[frame * height + piece * span : frame * height + (piece + 1) * span]
+        value = value.astype(F32).reshape(size, channels) + (totals[frame, piece] + offset_ref[...])
+        rows = pl.ds(piece * span, span)
+        out_ref[frame, rows] = value.astype(BF16).reshape(span, width, channels)
+        sends.append(pltpu.make_async_copy(
+            out_ref.at[frame, rows], out_hbm.at[frame, rows], sent.at[frame * pieces + piece]))
+        sends[-1].start()
+
     for which in range(4):
         prepare(which)
-    for frame in range(frames):
-        total = jnp.zeros((height * width, channels), F32)
-        for lagged in range(3):
-            for vertical in range(3):
-                at = ((frame + lagged) * (height + 2) + vertical) * width
-                total = total + jnp.dot(
-                    shifted[at : at + height * width, :],
-                    taps_ref[lagged * 3 + vertical],
-                    preferred_element_type=F32,
-                )
-        value = own_ref[frame * height : (frame + 1) * height].astype(F32).reshape(height * width, channels)
-        value = value + (total + offset_ref[...])
-        out_ref[frame] = value.astype(BF16).reshape(height, width, channels)
+        gather(which)
+    for send in sends:
+        send.wait()
 
 
 def convolve(sums, past, own, gain, shift, offset, taps, shape):
     frames, height, width, channels = shape
     return pl.pallas_call(
         conv_kernel,
-        out_shape=jax.ShapeDtypeStruct(shape, BF16),
+        out_shape=pltpu.HBM(shape, BF16),
         in_specs=[VMEM] * 7,
-        out_specs=VMEM,
+        out_specs=AWAY,
         scratch_shapes=[
             pltpu.VMEM((4 * (height + 2) * width, 3 * channels), BF16),
+            pltpu.VMEM(shape, BF16),
+            pltpu.SemaphoreType.DMA((4 * frames,)),
         ],
         compiler_params=pltpu.CompilerParams(vmem_limit_bytes=32 << 20),
         cost_estimate=pl.CostEstimate(flops=4 << 30, bytes_accessed=6 << 20, transcendentals=1 << 20),

time: 55.6 us -> 54.8 us (0.986)
  no operation moved by 1% of the time
where the time goes in v4:
time: 54.8 us; the launch traced here: 54.7 us
  blocking collectives  44.5 us (81%)
  Pallas kernels  6.57 us (12%)
  starting transfers between devices  3.52 us (6%)
    all_to_all x1, blocking collectives, local(): sums = lax.all_to_all(sums, 'tm', 0, 0).reshape(times, 128)  20.4 us
    all_to_all x1, blocking collectives, local(): rows = lax.all_to_all(rows, 'space', 0, 0, axis_index_groups=along)  15.4 us
    all_gather x1, blocking collectives, local(): sides = lax.all_gather(columns, 'space', axis_index_groups=across)  8.75 us
    pallas_call x1, Pallas kernels, convolve(): pl.pallas_call(conv_kernel, out_shape=pltpu.HBM(shape, BF16), in_specs=[V...  4.97 us
    ppermute x1, starting transfers between devices, local(): past = lax.ppermute(message, 'tm', later)  3.52 us
    pallas_call x1, Pallas kernels, group_sums(): pl.pallas_call(functools.partial(sums_kernel, frames=count), out_shape=[j...  1.53 us
  transfers between devices with their start and end apart: 1, of which 0 were waited for; matrix products, arithmetic and copies ran while one was open for 0% of the time, Pallas kernels for 0%

profile of v4, /device:TPU:64, one launch (start us, length us, event | category | flops | bytes accessed | tf_op | source)
XLA Modules:
  0.0 54.7 jit_solution(13325907101228400990)
XLA Ops:
  0.0 0.0 copy-start
  0.0 1.5 %shard_map.55 = (bf16[39,32,256]{2,1,0:T(8,128)(2,1)S(1)}, bf16[80,256]{1,0:T(8,128)(2,1)S(1)}, f32[1,256]{1,0:T(1,128)S(1)}, f32[1,256]{1,0:T(1,128)S(1)}, f32[1,256]{1,0:T(1,128)S(1)}) custom-call(bf16[32,32,256]{2,1,0:T(8,128)(2,1)} %bitcast.15, f32[1,256]{1,0:T(1,128)} %bitcast.16, f32[1,256]{1,0:T(1,128)} %bitcast.17, f32[1,256]{1,0:T(1,128)} %bitcast.18), custom_call_target="tpu_custom_call" | custom-call | flops 1048576 | bytes 131072 | tf_op jit(solution)/shard_map/pallas_call | solution.py:105
  1.5 8.7 %all-gather = bf16[320,256]{1,0:T(8,128)(2,1)S(1)} all-gather(bf16[80,256]{1,0:T(8,128)(2,1)S(1)} %get-tuple-element.13), channel_id=2, replica_groups={{0,1,2,3},{4,5,6,7},{8,9,10,11},{12,13,14,15},{16,17,18,19},{20,21,22,2..., dimensions={0}, use_global_device_ids=true | all-gather | bytes 204800 | tf_op jit(solution)/shard_map/all_gather | solution.py:347
  10.3 15.4 %all_to_all.10.rows_ref = bf16[4,80,256]{2,1,0:T(8,128)(2,1)S(1)} all-to-all(bf16[4,80,256]{2,1,0:T(8,128)(2,1)S(1)} %shard_map.56), channel_id=1, replica_groups={{0,4,8,12},{1,5,9,13},{2,6,10,14},{3,7,11,15},{16,20,24,28},{17,21,25,2..., dimensions={0} | all-to-all | bytes 327680 | tf_op jit(solution)/shard_map/all_to_all | solution.py:350
  25.8 3.5 %collective-permute-start = (bf16[39,32,256]{2,1,0:T(8,128)(2,1)S(1)}, bf16[39,32,256]{2,1,0:T(8,128)(2,1)S(1)}, u32[]{:S(2)}, u32[]{:S(2)}) collective-permute-start(bf16[39,32,256]{2,1,0:T(8,128)(2,1)S(1)} %get-tuple-element.15.own_ref), channel_id=1, source_target_pairs={{0,16},{16,32},{32,48},{48,64},{64,80},{80,96},{96,112},{112,128},... | collective-permute-start | bytes 1916936 | tf_op jit(solution)/shard_map/ppermute | solution.py:352
  29.3 20.4 %all_to_all.11 = f32[32,1,128]{2,1,0:T(1,128)S(1)} all-to-all(f32[32,1,128]{2,1,0:T(1,128)S(1)} %get-tuple-element.14), channel_id=1, replica_groups=mesh['tm'=32,'space'=16] {'tm'}, dimensions={0} | all-to-all | bytes 32768 | tf_op jit(solution)/shard_map/all_to_all | solution.py:353
  49.7 0.0 collective-permute-done.past_ref
  49.7 0.0 copy-done
  49.7 5.0 %shard_map.58 = bf16[2,16,32,256]{3,2,1,0:T(8,128)(2,1)} custom-call(f32[32,128]{1,0:T(8,128)S(1)} %bitcast.14, bf16[39,32,256]{2,1,0:T(8,128)(2,1)S(1)} %collective-permute-done.past_ref, bf16[39,32,256]{2,1,0:T(8,128)(2,1)S(1)} %get-tuple-element.15.own_ref, f32[1,256]{1,0:T(1,128)S(1)} %get-tuple-element.16.gain_ref, ...), custom_call_target="tpu_custom_call" | custom-call | flops 4294967296 | bytes 6291456 | tf_op jit(solution)/shard_map/pallas_call | solution.py:322
  (2 shorter events, 0.1 us)
Async XLA Ops:
  0.0 49.7 %copy-start = (bf16[3,3,3,256,256]{4,3,2,1,0:T(8,128)(2,1)S(1)}, bf16[3,3,3,256,256]{4,3,2,1,0:T(8,128)(2,1)}, u32[]{:S(2)}) copy-start(bf16[3,3,3,256,256]{4,3,2,1,0:T(8,128)(2,1)} %param.8) | copy-start | bytes 10616836
  25.8 23.9 %collective-permute-start = (bf16[39,32,256]{2,1,0:T(8,128)(2,1)S(1)}, bf16[39,32,256]{2,1,0:T(8,128)(2,1)S(1)}, u32[]{:S(2)}, u32[]{:S(2)}) collective-permute-start(bf16[39,32,256]{2,1,0:T(8,128)(2,1)S(1)} %get-tuple-element.15.own_ref), channel_id=1, source_target_pairs={{0,16},{16,32},{32,48},{48,64},{64,80},{80,96},{96,112},{112,128},... | collective-permute-start | bytes 1916936 | tf_op jit(solution)/shard_map/ppermute | solution.py:352

commit v5 on v4

--- a/solution.py
+++ b/solution.py
@@ -42,16 +42,15 @@
 
 
 def split_rows(row):
-    high, middle, low = (part.astype(F32) for part in split(row))
-    upper = jnp.concatenate([high, middle], axis=1)
-    lower = jnp.concatenate([low, jnp.zeros_like(low)], axis=1)
-    place = lax.broadcasted_iota(jnp.int32, (16, upper.shape[1]), 0)
-    return jnp.where(place == 0, upper, jnp.where(place == 1, lower, 0.0))
+    place = lax.broadcasted_iota(jnp.int32, (16, 128), 0)
+    block = jnp.zeros((16, 128), F32)
+    for at, part in enumerate(split(row)):
+        block = jnp.where(place == at, part.astype(F32), block)
+    return block
 
 
 def joined_row(block):
-    upper, lower = block[0:1], block[1:2]
-    return upper[:, :128] + upper[:, 128:] + lower[:, :128]
+    return block[0:1] + block[1:2] + block[2:3]
 
 
 def sums_kernel(frames_hbm, gain_hbm, shift_hbm, offset_hbm, message_ref, columns_ref, gain_ref, shift_ref,
@@ -90,10 +89,11 @@
             square = square + (block * block).sum(0)
         plains.append(plain)
         squares.append(square)
-        columns_ref[frame * height : (frame + 1) * height] = jnp.concatenate(firsts, axis=0).astype(BF16)
-        columns_ref[rows + frame * height : rows + (frame + 1) * height] = jnp.concatenate(lasts, axis=0).astype(BF16)
+        columns_ref[:, frame * channels : (frame + 1) * channels] = jnp.concatenate(firsts, axis=0).astype(BF16)
+        at = (frames + frame) * channels
+        columns_ref[:, at : at + channels] = jnp.concatenate(lasts, axis=0).astype(BF16)
     total = exact_dot(jnp.concatenate(plains + squares, axis=1), table)
-    columns_ref[2 * rows : 2 * rows + 16] = split_rows(total.sum(0, keepdims=True)).astype(BF16)
+    columns_ref[:, 2 * frames * channels :] = split_rows(total.sum(0, keepdims=True)).astype(BF16)
     for fetch in fetches[4:]:
         fetch.wait()
 
@@ -106,7 +106,7 @@
         functools.partial(sums_kernel, frames=count),
         out_shape=[
             jax.ShapeDtypeStruct((rows + 3 * count + 1, width, channels), BF16),
-            jax.ShapeDtypeStruct((2 * rows + 16, channels), BF16),
+            jax.ShapeDtypeStruct((height, 2 * count * channels + 128), BF16),
             vector,
             vector,
             vector,
@@ -126,35 +126,41 @@
 def rows_kernel(message_ref, sides_ref, taps_hbm, out_ref, *, frames, height):
     width, channels = message_ref.shape[1:]
     members, receivers = sides_ref.shape[0], out_ref.shape[0]
-    rows = frames * height
     tile = lax.axis_index("space")
     row_of, col_of = tile // ACROSS, tile % ACROSS
     on_left, on_right = beside(col_of, -1, members), beside(col_of, 1, members)
+    ends_at = 2 * frames * channels
     total = jnp.zeros((1, 128), F32)
     for member in range(members):
-        total = total + joined_row(sides_ref[member, 2 * rows : 2 * rows + 16].astype(F32))
+        total = total + joined_row(sides_ref[member, :, ends_at : ends_at + 128].astype(F32))
     upper = lower = split_rows(total)
-    place = lax.broadcasted_iota(jnp.int32, (16, channels), 0)
+    place = lax.broadcasted_iota(jnp.int32, (16, 128), 0)
     for frame in range(frames):
-        left = sides_ref[on_left, rows + frame * height : rows + (frame + 1) * height].astype(F32)
-        right = sides_ref[on_right, frame * height : (frame + 1) * height].astype(F32)
+        begin = (frames + frame) * channels
+        left = sides_ref[on_left, :, begin : begin + channels].astype(F32)
+        right = sides_ref[on_right, :, frame * channels : (frame + 1) * channels].astype(F32)
         for at, side in enumerate((left, right)):
-            upper = jnp.where(place == 2 + 2 * frame + at, side[0:1], upper)
-            lower = jnp.where(place == 2 + 2 * frame + at, side[height - 1 : height], lower)
+            for half in range(2):
+                row = place == 3 + 4 * frame + 2 * at + half
+                lanes = slice(half * 128, (half + 1) * 128)
+                upper = jnp.where(row, side[0:1, lanes], upper)
+                lower = jnp.where(row, side[height - 1 : height, lanes], lower)
     for receiver in range(receivers):
         is_above = receiver < row_of
         for frame in range(frames):
             row = frame * height + jnp.where(is_above, 0, height - 1)
-            out_ref[receiver, frame * width : (frame + 1) * width] = message_ref[row]
+            for half in range(2):
+                begin = (2 * frame + half) * channels
+                out_ref[receiver, :, begin : begin + channels] = message_ref[row, half * 16 : half * 16 + 16]
         ends = jnp.where(is_above, upper, lower)
-        out_ref[receiver, frames * width : frames * width + 16] = ends.astype(BF16)
+        out_ref[receiver, :, ends_at : ends_at + 128] = ends.astype(BF16)
 
 
 def edge_rows(message, sides, taps, frames, height, receivers):
     width, channels = message.shape[1:]
     return pl.pallas_call(
         functools.partial(rows_kernel, frames=frames, height=height),
-        out_shape=jax.ShapeDtypeStruct((receivers, frames * width + 16, channels), BF16),
+        out_shape=jax.ShapeDtypeStruct((receivers, width // 2, 2 * frames * channels + 128), BF16),
         in_specs=[VMEM, VMEM, AWAY],
         out_specs=VMEM,
         compiler_params=SMALL,
@@ -170,23 +176,27 @@
     row_of, col_of = tile // ACROSS, tile % ACROSS
     on_left, on_right = beside(col_of, -1, across), beside(col_of, 1, across)
     above, below = beside(row_of, -1, members), beside(row_of, 1, members)
-    ends_at = frames * width
+    ends_at = 2 * frames * channels
     total = jnp.zeros((1, 128), F32)
     for member in range(members):
-        total = total + joined_row(rows_ref[member, ends_at : ends_at + 16].astype(F32))
+        total = total + joined_row(rows_ref[member, :, ends_at : ends_at + 128].astype(F32))
     sums_ref[...] = jnp.broadcast_to(total[None], sums_ref.shape)
-    upper = rows_ref[above, ends_at : ends_at + 16].astype(F32)
-    lower = rows_ref[below, ends_at : ends_at + 16].astype(F32)
+    upper = rows_ref[above, :, ends_at : ends_at + 128].astype(F32)
+    lower = rows_ref[below, :, ends_at : ends_at + 128].astype(F32)
     place = lax.broadcasted_iota(jnp.int32, (16, channels), 0)
     corners = jnp.zeros((16, channels), F32)
     for frame in range(frames):
         at = rows + 3 * frame
-        out_ref[at, 0:height] = sides_ref[on_left, rows + frame * height : rows + (frame + 1) * height]
-        out_ref[at, height : 2 * height] = sides_ref[on_right, frame * height : (frame + 1) * height]
-        out_ref[at + 1] = rows_ref[above, frame * width : (frame + 1) * width]
-        out_ref[at + 2] = rows_ref[below, frame * width : (frame + 1) * width]
-        base = 2 + 2 * frame
-        cells = (upper[base : base + 1], lower[base : base + 1], upper[base + 1 : base + 2], lower[base + 1 : base + 2])
+        out_ref[at, 0:height] = sides_ref[on_left, :, (frames + frame) * channels : (frames + frame + 1) * channels]
+        out_ref[at, height : 2 * height] = sides_ref[on_right, :, frame * channels : (frame + 1) * channels]
+        for half in range(2):
+            begin = (2 * frame + half) * channels
+            out_ref[at + 1, half * 16 : half * 16 + 16] = rows_ref[above, :, begin : begin + channels]
+            out_ref[at + 2, half * 16 : half * 16 + 16] = rows_ref[below, :, begin : begin + channels]
+        cells = []
+        for base in (3 + 4 * frame, 5 + 4 * frame):
+            for block in (upper, lower):
+                cells.append(jnp.concatenate([block[base : base + 1], block[base + 1 : base + 2]], axis=1))
         for index, cell in enumerate(cells):
             corners = jnp.where(place == 4 * frame + index, cell, corners)
     out_ref[rows + 3 * frames, 0:16] = corners.astype(BF16)

time: 54.8 us -> 54.3 us (level)
  no operation moved by 1% of the time
where the time goes in v5:
time: 54.3 us; the launch traced here: 54.1 us
  blocking collectives  44 us (81%)
  Pallas kernels  6.56 us (12%)
  starting transfers between devices  3.52 us (6%)
    all_to_all x1, blocking collectives, local(): sums = lax.all_to_all(sums, 'tm', 0, 0).reshape(times, 128)  20.1 us
    all_to_all x1, blocking collectives, local(): rows = lax.all_to_all(rows, 'space', 0, 0, axis_index_groups=along)  15.2 us
    all_gather x1, blocking collectives, local(): sides = lax.all_gather(columns, 'space', axis_index_groups=across)  8.66 us
    pallas_call x1, Pallas kernels, convolve(): pl.pallas_call(conv_kernel, out_shape=pltpu.HBM(shape, BF16), in_specs=[V...  4.97 us
    ppermute x1, starting transfers between devices, local(): past = lax.ppermute(message, 'tm', later)  3.52 us
    pallas_call x1, Pallas kernels, group_sums(): pl.pallas_call(functools.partial(sums_kernel, frames=count), out_shape=[j...  1.53 us
  transfers between devices with their start and end apart: 1, of which 0 were waited for; matrix products, arithmetic and copies ran while one was open for 0% of the time, Pallas kernels for 0%

profile of v5, /device:TPU:64, one launch (start us, length us, event | category | flops | bytes accessed | tf_op | source)
XLA Modules:
  0.0 54.1 jit_solution(13723860763801035978)
XLA Ops:
  0.0 0.0 copy-start
  0.0 1.5 %shard_map.55 = (bf16[39,32,256]{2,1,0:T(8,128)(2,1)S(1)}, bf16[16,1152]{1,0:T(8,128)(2,1)S(1)}, f32[1,256]{1,0:T(1,128)S(1)}, f32[1,256]{1,0:T(1,128)S(1)}, f32[1,256]{1,0:T(1,128)S(1)}) custom-call(bf16[32,32,256]{2,1,0:T(8,128)(2,1)} %bitcast.15, f32[1,256]{1,0:T(1,128)} %bitcast.16, f32[1,256]{1,0:T(1,128)} %bitcast.17, f32[1,256]{1,0:T(1,128)} %bitcast.18), custom_call_target="tpu_custom_call" | custom-call | flops 1048576 | bytes 131072 | tf_op jit(solution)/shard_map/pallas_call | solution.py:105
  1.5 8.7 %all-gather = bf16[64,1152]{1,0:T(8,128)(2,1)S(1)} all-gather(bf16[16,1152]{1,0:T(8,128)(2,1)S(1)} %get-tuple-element.13), channel_id=2, replica_groups={{0,1,2,3},{4,5,6,7},{8,9,10,11},{12,13,14,15},{16,17,18,19},{20,21,22,2..., dimensions={0}, use_global_device_ids=true | all-gather | bytes 184320 | tf_op jit(solution)/shard_map/all_gather | solution.py:357
  10.2 15.2 %all_to_all.10.rows_ref = bf16[4,16,1152]{2,1,0:T(8,128)(2,1)S(1)} all-to-all(bf16[4,16,1152]{2,1,0:T(8,128)(2,1)S(1)} %shard_map.56), channel_id=1, replica_groups={{0,4,8,12},{1,5,9,13},{2,6,10,14},{3,7,11,15},{16,20,24,28},{17,21,25,2..., dimensions={0} | all-to-all | bytes 294912 | tf_op jit(solution)/shard_map/all_to_all | solution.py:360
  25.5 3.5 %collective-permute-start = (bf16[39,32,256]{2,1,0:T(8,128)(2,1)S(1)}, bf16[39,32,256]{2,1,0:T(8,128)(2,1)S(1)}, u32[]{:S(2)}, u32[]{:S(2)}) collective-permute-start(bf16[39,32,256]{2,1,0:T(8,128)(2,1)S(1)} %get-tuple-element.15.own_ref), channel_id=1, source_target_pairs={{0,16},{16,32},{32,48},{48,64},{64,80},{80,96},{96,112},{112,128},... | collective-permute-start | bytes 1916936 | tf_op jit(solution)/shard_map/ppermute | solution.py:362
  29.0 20.1 %all_to_all.11 = f32[32,1,128]{2,1,0:T(1,128)S(1)} all-to-all(f32[32,1,128]{2,1,0:T(1,128)S(1)} %get-tuple-element.14), channel_id=1, replica_groups=mesh['tm'=32,'space'=16] {'tm'}, dimensions={0} | all-to-all | bytes 32768 | tf_op jit(solution)/shard_map/all_to_all | solution.py:363
  49.1 0.0 collective-permute-done.past_ref
  49.1 0.0 copy-done
  49.1 5.0 %shard_map.58 = bf16[2,16,32,256]{3,2,1,0:T(8,128)(2,1)} custom-call(f32[32,128]{1,0:T(8,128)S(1)} %bitcast.14, bf16[39,32,256]{2,1,0:T(8,128)(2,1)S(1)} %collective-permute-done.past_ref, bf16[39,32,256]{2,1,0:T(8,128)(2,1)S(1)} %get-tuple-element.15.own_ref, f32[1,256]{1,0:T(1,128)S(1)} %get-tuple-element.16.gain_ref, ...), custom_call_target="tpu_custom_call" | custom-call | flops 4294967296 | bytes 6291456 | tf_op jit(solution)/shard_map/pallas_call | solution.py:332
  (2 shorter events, 0.1 us)
Async XLA Ops:
  0.0 49.1 %copy-start = (bf16[3,3,3,256,256]{4,3,2,1,0:T(8,128)(2,1)S(1)}, bf16[3,3,3,256,256]{4,3,2,1,0:T(8,128)(2,1)}, u32[]{:S(2)}) copy-start(bf16[3,3,3,256,256]{4,3,2,1,0:T(8,128)(2,1)} %param.8) | copy-start | bytes 10616836
  25.5 23.6 %collective-permute-start = (bf16[39,32,256]{2,1,0:T(8,128)(2,1)S(1)}, bf16[39,32,256]{2,1,0:T(8,128)(2,1)S(1)}, u32[]{:S(2)}, u32[]{:S(2)}) collective-permute-start(bf16[39,32,256]{2,1,0:T(8,128)(2,1)S(1)} %get-tuple-element.15.own_ref), channel_id=1, source_target_pairs={{0,16},{16,32},{32,48},{48,64},{64,80},{80,96},{96,112},{112,128},... | collective-permute-start | bytes 1916936 | tf_op jit(solution)/shard_map/ppermute | solution.py:362

commit v6 on v5

--- a/solution.py
+++ b/solution.py
@@ -55,20 +55,21 @@
 
 def sums_kernel(frames_hbm, gain_hbm, shift_hbm, offset_hbm, message_ref, columns_ref, gain_ref, shift_ref,
                 offset_ref, arrived, *, frames):
-    rows, width, channels = frames_hbm.shape
+    blocks, half, channels = frames_hbm.shape
+    rows, width = blocks // 2, 2 * half
     height = rows // frames
     per_group = channels // GROUPS
     part = rows // 4
     fetches = []
     for at in range(4):
-        span = pl.ds(at * part, part)
+        span = pl.ds(at * 2 * part, 2 * part)
         fetches.append(pltpu.make_async_copy(frames_hbm.at[span], message_ref.at[span], arrived.at[at]))
         fetches[-1].start()
     small = ((gain_hbm, gain_ref), (shift_hbm, shift_ref), (offset_hbm, offset_ref))
     for at, (source, target) in enumerate(small):
         fetches.append(pltpu.make_async_copy(source, target, arrived.at[4 + at]))
         fetches[-1].start()
-    message_ref[rows:] = jnp.zeros((message_ref.shape[0] - rows, width, channels), BF16)
+    message_ref[blocks:] = jnp.zeros((message_ref.shape[0] - blocks, half, channels), BF16)
     kinds = 2 * frames
     source = lax.broadcasted_iota(jnp.int32, (kinds * channels, 128), 0)
     lane = lax.broadcasted_iota(jnp.int32, (kinds * channels, 128), 1)
@@ -81,7 +82,7 @@
         for row in range(frame * height, (frame + 1) * height):
             if row % part == 0:
                 fetches[row // part].wait()
-            block = message_ref[row].astype(F32)
+            block = message_ref[2 * row : 2 * row + 2].astype(F32).reshape(width, channels)
             firsts.append(block[0:1])
             lasts.append(block[width - 1 : width])
             block = block.reshape(width // 8, 8, channels)
@@ -105,7 +106,7 @@
     return pl.pallas_call(
         functools.partial(sums_kernel, frames=count),
         out_shape=[
-            jax.ShapeDtypeStruct((rows + 3 * count + 1, width, channels), BF16),
+            jax.ShapeDtypeStruct((2 * rows + 6 * count + 1, width // 2, channels), BF16),
             jax.ShapeDtypeStruct((height, 2 * count * channels + 128), BF16),
             vector,
             vector,
@@ -116,7 +117,7 @@
         scratch_shapes=[pltpu.SemaphoreType.DMA((7,))],
         compiler_params=SMALL,
         cost_estimate=cost(1 << 20),
-    )(in_hbm(own.reshape(rows, width, channels)), in_hbm(gain), in_hbm(shift), in_hbm(offset))
+    )(in_hbm(own.reshape(2 * rows, width // 2, channels)), in_hbm(gain), in_hbm(shift), in_hbm(offset))
 
 
 def beside(index, step, count):
@@ -124,7 +125,7 @@
 
 
 def rows_kernel(message_ref, sides_ref, taps_hbm, out_ref, *, frames, height):
-    width, channels = message_ref.shape[1:]
+    channels = message_ref.shape[2]
     members, receivers = sides_ref.shape[0], out_ref.shape[0]
     tile = lax.axis_index("space")
     row_of, col_of = tile // ACROSS, tile % ACROSS
@@ -151,13 +152,13 @@
             row = frame * height + jnp.where(is_above, 0, height - 1)
             for half in range(2):
                 begin = (2 * frame + half) * channels
-                out_ref[receiver, :, begin : begin + channels] = message_ref[row, half * 16 : half * 16 + 16]
+                out_ref[receiver, :, begin : begin + channels] = message_ref[2 * row + half]
         ends = jnp.where(is_above, upper, lower)
         out_ref[receiver, :, ends_at : ends_at + 128] = ends.astype(BF16)
 
 
 def edge_rows(message, sides, taps, frames, height, receivers):
-    width, channels = message.shape[1:]
+    width, channels = 2 * message.shape[1], message.shape[2]
     return pl.pallas_call(
         functools.partial(rows_kernel, frames=frames, height=height),
         out_shape=jax.ShapeDtypeStruct((receivers, width // 2, 2 * frames * channels + 128), BF16),
@@ -169,7 +170,7 @@
 
 
 def border_kernel(message_ref, sides_ref, rows_ref, out_ref, sums_ref, *, frames, height):
-    width, channels = message_ref.shape[1:]
+    channels = message_ref.shape[2]
     members, across = rows_ref.shape[0], sides_ref.shape[0]
     rows = frames * height
     tile = lax.axis_index("space")
@@ -186,20 +187,20 @@
     place = lax.broadcasted_iota(jnp.int32, (16, channels), 0)
     corners = jnp.zeros((16, channels), F32)
     for frame in range(frames):
-        at = rows + 3 * frame
-        out_ref[at, 0:height] = sides_ref[on_left, :, (frames + frame) * channels : (frames + frame + 1) * channels]
-        out_ref[at, height : 2 * height] = sides_ref[on_right, :, frame * channels : (frame + 1) * channels]
+        at = 2 * rows + 6 * frame
+        out_ref[at] = sides_ref[on_left, :, (frames + frame) * channels : (frames + frame + 1) * channels]
+        out_ref[at + 1] = sides_ref[on_right, :, frame * channels : (frame + 1) * channels]
         for half in range(2):
             begin = (2 * frame + half) * channels
-            out_ref[at + 1, half * 16 : half * 16 + 16] = rows_ref[above, :, begin : begin + channels]
-            out_ref[at + 2, half * 16 : half * 16 + 16] = rows_ref[below, :, begin : begin + channels]
+            out_ref[at + 2 + half] = rows_ref[above, :, begin : begin + channels]
+            out_ref[at + 4 + half] = rows_ref[below, :, begin : begin + channels]
         cells = []
         for base in (3 + 4 * frame, 5 + 4 * frame):
             for block in (upper, lower):
                 cells.append(jnp.concatenate([block[base : base + 1], block[base + 1 : base + 2]], axis=1))
         for index, cell in enumerate(cells):
             corners = jnp.where(place == 4 * frame + index, cell, corners)
-    out_ref[rows + 3 * frames, 0:16] = corners.astype(BF16)
+    out_ref[2 * rows + 6 * frames] = corners.astype(BF16)
 
 
 def add_border(message, sides, rows, frames, height, receivers):
@@ -275,17 +276,18 @@
         source = past_ref if which < 2 else own_ref
         here = has_past if which < 2 else jnp.ones((), F32)
         frame = which % 2
-        at = rows + 3 * frame
-        left = activate(source[at, 0:height], which) * (has_left * here)
-        right = activate(source[at, height : 2 * height], which) * (has_right * here)
-        up = activate(source[at + 1], which) * (has_up * here)
-        down = activate(source[at + 2], which) * (has_down * here)
-        corners = activate(source[rows + 3 * frames, 0:16], which) * here
+        at = 2 * rows + 6 * frame
+        left = activate(source[at], which) * (has_left * here)
+        right = activate(source[at + 1], which) * (has_right * here)
+        up = activate(source[at + 2 : at + 4].reshape(width, channels), which) * (has_up * here)
+        down = activate(source[at + 4 : at + 6].reshape(width, channels), which) * (has_down * here)
+        corners = activate(source[2 * rows + 6 * frames], which) * here
         corners = corners[4 * frame : 4 * frame + 4]
         put(which, 0, up, corners[0:1] * (has_up * has_left), corners[2:3] * (has_up * has_right))
         put(which, height + 1, down, corners[1:2] * (has_down * has_left), corners[3:4] * (has_down * has_right))
         for row in range(height):
-            center = activate(source[frame * height + row], which)
+            begin = 2 * (frame * height + row)
+            center = activate(source[begin : begin + 2].reshape(width, channels), which)
             if which < 2:
                 center = center * here
             put(which, row + 1, center, left[row : row + 1], right[row : row + 1])
@@ -312,7 +314,8 @@
 
     def finish(frame, piece):
         span = height // pieces
-        value = own_ref[frame * height + piece * span : frame * height + (piece + 1) * span]
+        begin = 2 * (frame * height + piece * span)
+        value = own_ref[begin : begin + 2 * span]
         value = value.astype(F32).reshape(size, channels) + (totals[frame, piece] + offset_ref[...])
         rows = pl.ds(piece * span, span)
         out_ref[frame, rows] = value.astype(BF16).reshape(span, width, channels)

time: 54.3 us -> 54.1 us (level)
  no operation moved by 1% of the time
where the time goes in v6:
time: 54.1 us; the launch traced here: 53.9 us
  blocking collectives  43.8 us (81%)
  Pallas kernels  6.61 us (12%)
  starting transfers between devices  3.52 us (7%)
    all_to_all x1, blocking collectives, local(): sums = lax.all_to_all(sums, 'tm', 0, 0).reshape(times, 128)  19.9 us
    all_to_all x1, blocking collectives, local(): rows = lax.all_to_all(rows, 'space', 0, 0, axis_index_groups=along)  15.2 us
    all_gather x1, blocking collectives, local(): sides = lax.all_gather(columns, 'space', axis_index_groups=across)  8.66 us
    pallas_call x1, Pallas kernels, convolve(): pl.pallas_call(conv_kernel, out_shape=pltpu.HBM(shape, BF16), in_specs=[V...  5.01 us
    ppermute x1, starting transfers between devices, local(): past = lax.ppermute(message, 'tm', later)  3.52 us
    pallas_call x1, Pallas kernels, group_sums(): pl.pallas_call(functools.partial(sums_kernel, frames=count), out_shape=[j...  1.53 us
  transfers between devices with their start and end apart: 1, of which 0 were waited for; matrix products, arithmetic and copies ran while one was open for 0% of the time, Pallas kernels for 0%

profile of v6, /device:TPU:64, one launch (start us, length us, event | category | flops | bytes accessed | tf_op | source)
XLA Modules:
  0.0 53.9 jit_solution(3009176509768039717)
XLA Ops:
  0.0 0.0 copy-start
  0.0 1.5 %shard_map.55 = (bf16[77,16,256]{2,1,0:T(8,128)(2,1)S(1)}, bf16[16,1152]{1,0:T(8,128)(2,1)S(1)}, f32[1,256]{1,0:T(1,128)S(1)}, f32[1,256]{1,0:T(1,128)S(1)}, f32[1,256]{1,0:T(1,128)S(1)}) custom-call(bf16[64,16,256]{2,1,0:T(8,128)(2,1)} %bitcast.15, f32[1,256]{1,0:T(1,128)} %bitcast.16, f32[1,256]{1,0:T(1,128)} %bitcast.17, f32[1,256]{1,0:T(1,128)} %bitcast.18), custom_call_target="tpu_custom_call" | custom-call | flops 1048576 | bytes 131072 | tf_op jit(solution)/shard_map/pallas_call | solution.py:106
  1.5 8.7 %all-gather = bf16[64,1152]{1,0:T(8,128)(2,1)S(1)} all-gather(bf16[16,1152]{1,0:T(8,128)(2,1)S(1)} %get-tuple-element.13), channel_id=2, replica_groups={{0,1,2,3},{4,5,6,7},{8,9,10,11},{12,13,14,15},{16,17,18,19},{20,21,22,2..., dimensions={0}, use_global_device_ids=true | all-gather | bytes 184320 | tf_op jit(solution)/shard_map/all_gather | solution.py:360
  10.2 15.2 %all_to_all.10.rows_ref = bf16[4,16,1152]{2,1,0:T(8,128)(2,1)S(1)} all-to-all(bf16[4,16,1152]{2,1,0:T(8,128)(2,1)S(1)} %shard_map.56), channel_id=1, replica_groups={{0,4,8,12},{1,5,9,13},{2,6,10,14},{3,7,11,15},{16,20,24,28},{17,21,25,2..., dimensions={0} | all-to-all | bytes 294912 | tf_op jit(solution)/shard_map/all_to_all | solution.py:363
  25.5 3.5 %collective-permute-start = (bf16[77,16,256]{2,1,0:T(8,128)(2,1)S(1)}, bf16[77,16,256]{2,1,0:T(8,128)(2,1)S(1)}, u32[]{:S(2)}, u32[]{:S(2)}) collective-permute-start(bf16[77,16,256]{2,1,0:T(8,128)(2,1)S(1)} %get-tuple-element.15.own_ref), channel_id=1, source_target_pairs={{0,16},{16,32},{32,48},{48,64},{64,80},{80,96},{96,112},{112,128},... | collective-permute-start | bytes 1892360 | tf_op jit(solution)/shard_map/ppermute | solution.py:365
  29.0 19.9 %all_to_all.11 = f32[32,1,128]{2,1,0:T(1,128)S(1)} all-to-all(f32[32,1,128]{2,1,0:T(1,128)S(1)} %get-tuple-element.14), channel_id=1, replica_groups=mesh['tm'=32,'space'=16] {'tm'}, dimensions={0} | all-to-all | bytes 32768 | tf_op jit(solution)/shard_map/all_to_all | solution.py:366
  48.9 0.0 collective-permute-done.past_ref
  48.9 0.0 copy-done
  48.9 5.0 %shard_map.58 = bf16[2,16,32,256]{3,2,1,0:T(8,128)(2,1)} custom-call(f32[32,128]{1,0:T(8,128)S(1)} %bitcast.14, bf16[77,16,256]{2,1,0:T(8,128)(2,1)S(1)} %collective-permute-done.past_ref, bf16[77,16,256]{2,1,0:T(8,128)(2,1)S(1)} %get-tuple-element.15.own_ref, f32[1,256]{1,0:T(1,128)S(1)} %get-tuple-element.16.gain_ref, ...), custom_call_target="tpu_custom_call" | custom-call | flops 4294967296 | bytes 6291456 | tf_op jit(solution)/shard_map/pallas_call | solution.py:335
  (2 shorter events, 0.1 us)
Async XLA Ops:
  0.0 48.9 %copy-start = (bf16[3,3,3,256,256]{4,3,2,1,0:T(8,128)(2,1)S(1)}, bf16[3,3,3,256,256]{4,3,2,1,0:T(8,128)(2,1)}, u32[]{:S(2)}) copy-start(bf16[3,3,3,256,256]{4,3,2,1,0:T(8,128)(2,1)} %param.8) | copy-start | bytes 10616836
  25.5 23.4 %collective-permute-start = (bf16[77,16,256]{2,1,0:T(8,128)(2,1)S(1)}, bf16[77,16,256]{2,1,0:T(8,128)(2,1)S(1)}, u32[]{:S(2)}, u32[]{:S(2)}) collective-permute-start(bf16[77,16,256]{2,1,0:T(8,128)(2,1)S(1)} %get-tuple-element.15.own_ref), channel_id=1, source_target_pairs={{0,16},{16,32},{32,48},{48,64},{64,80},{80,96},{96,112},{112,128},... | collective-permute-start | bytes 1892360 | tf_op jit(solution)/shard_map/ppermute | solution.py:365
